TPU v7x, 128 devices: a whole 4x4x4 slice. The times are simulated.
128 devices in a mesh: heads: 4 (over y_hi, core), seq: 32 (over z, x, y_lo).
Axes of the slice: x: 4, y: 4 (y_hi: 2, y_lo: 2; y = y_hi * 2 + y_lo), z: 4, core: 2. Of those that a mesh axis runs over, the one named last changes fastest.
Arguments:
- queries: bfloat16 [65536, 8, 512], P('seq', 'heads'), may hold values from -6 to 6
- key_rows: bfloat16 [65536, 8, 512], P('seq', 'heads'), may hold values from -6 to 6
- value_rows: bfloat16 [65536, 8, 512], P('seq', 'heads'), may hold values from -6 to 6
- step_rates: bfloat16 [8, 65536], P('heads', 'seq'), may hold values from 0.25 to 4
- live_counts: int32 [32], replicated, may hold values from 256 to 2048, as said below
- group_scales: float32 [8], P('heads'), may hold values from 0.4 to 1.8
- w_first: float32 [8, 512, 512], P('heads', 'seq'), may hold values from -0.8838835 to 0.8838835
- w_third: float32 [8, 512, 512], P('heads', 'seq'), may hold values from -0.8838835 to 0.8838835
- w_second: float32 [8, 512, 512], P('heads', 'seq'), may hold values from -0.8838835 to 0.8838835
Outputs:
- fast_out: bfloat16 [65536, 8, 512], P('seq', 'heads')
Inputs may be any that keep to these rules, and one draw needn't show every extreme that they name: `live_counts`: live token count of each clip shard; every draw has one shard of 2048 live tokens.
All inputs are finite; a program needn't handle non-finite values.
Results may differ from a plain program's by a relative error of at most 0.012.
The roundings to bfloat16 on the way count: a program that leaves them out, or rounds other values in their place, can miss the bound.
Values may be sent and summed in bfloat16 or wider, within the bound.
No kernel may reach another device: no remote copies, remote signals or barrier semaphores. Data moves between devices by JAX's collectives and lax.ppermute only.
A program may use at most 128 MiB of HBM per device.

v0:
```python
import jax
import jax.numpy as jnp
from jax import lax
from jax.sharding import PartitionSpec as P

EPS = 1e-06


def row_normalize(start_w, update):
    norm_old = jnp.sqrt(jnp.mean(start_w * start_w, axis=-1, keepdims=True) + EPS)
    norm_new = jnp.sqrt(jnp.mean(update * update, axis=-1, keepdims=True) + EPS)
    return update * (norm_old / norm_new)


def group_terms(k_part, v_part, eta_col, b_one, b_three, b_two):
    h_one = jnp.dot(k_part, b_one, preferred_element_type=jnp.float32)
    h_three = jnp.dot(k_part, b_three, preferred_element_type=jnp.float32)
    gate = jax.nn.silu(h_one)
    act = (gate * h_three).astype(jnp.bfloat16)
    err = (eta_col[:, None] * v_part.astype(jnp.float32)).astype(jnp.bfloat16)
    back = jnp.dot(err, b_two.T, preferred_element_type=jnp.float32)
    sig = jax.nn.sigmoid(h_one)
    d_one = (back * h_three * (sig * (1.0 + h_one * (1.0 - sig)))).astype(jnp.bfloat16)
    d_three = (back * gate).astype(jnp.bfloat16)
    p_one = jnp.dot(k_part.T, d_one, preferred_element_type=jnp.float32)
    p_three = jnp.dot(k_part.T, d_three, preferred_element_type=jnp.float32)
    p_two = jnp.dot(act.T, err, preferred_element_type=jnp.float32)
    return (p_one, p_three, p_two)


def shard_terms(k_rows, v_rows, eta_rows, halves):
    b_one, b_three, b_two = halves
    firsts, thirds, seconds = ([], [], [])
    for group in range(k_rows.shape[1]):
        p_one, p_three, p_two = group_terms(
            k_rows[:, group],
            v_rows[:, group],
            eta_rows[:, group],
            b_one[group],
            b_three[group],
            b_two[group],
        )
        firsts.append(p_one)
        thirds.append(p_three)
        seconds.append(p_two)
    return (jnp.stack(firsts), jnp.stack(thirds), jnp.stack(seconds))


def apply_rows(q_rows, live_mask, fresh):
    c_one, c_three, c_two = fresh
    live_b = live_mask.astype(jnp.bfloat16)[:, None]
    pieces = []
    for group in range(q_rows.shape[1]):
        q_part = q_rows[:, group]
        q_one = jnp.dot(q_part, c_one[group], preferred_element_type=jnp.float32)
        q_three = jnp.dot(q_part, c_three[group], preferred_element_type=jnp.float32)
        a_query = (jax.nn.silu(q_one) * q_three).astype(jnp.bfloat16)
        o_part = jnp.dot(a_query, c_two[group], preferred_element_type=jnp.float32).astype(
            jnp.bfloat16
        )
        pieces.append(o_part * live_b)
    return jnp.stack(pieces, axis=1)


def shards(
    queries, key_rows, value_rows, step_rates, live_counts, group_scales, w_first, w_third, w_second
):
    cap_rows, groups, feat_width = queries.shape
    seq_size = lax.axis_size("seq")
    root_total = jnp.sqrt(jnp.float32(cap_rows * seq_size))
    own_index = lax.axis_index("seq")
    own_count = live_counts[own_index]
    position = jnp.arange(cap_rows, dtype=jnp.int32)
    live_mask = position < own_count
    full_rows = (
        lax.all_gather(w_first, "seq", axis=1, tiled=True),
        lax.all_gather(w_third, "seq", axis=1, tiled=True),
        lax.all_gather(w_second, "seq", axis=1, tiled=True),
    )
    halves = tuple((weight.astype(jnp.bfloat16) for weight in full_rows))
    eta_rows = (
        step_rates.T.astype(jnp.float32) * live_mask.astype(jnp.float32)[:, None] / root_total
    )
    sums = shard_terms(key_rows, value_rows, eta_rows, halves)
    summed = lax.psum((sums[0], sums[1], sums[2]), "seq")
    fresh = tuple(
        (
            row_normalize(weight, weight + term).astype(jnp.bfloat16)
            for weight, term in zip(full_rows, summed)
        )
    )
    fast = apply_rows(queries, live_mask, fresh)
    wide = fast.astype(jnp.float32) * group_scales[None, :, None]
    partial_sq = jnp.sum(wide * wide, axis=(1, 2))
    total_sq = lax.psum(partial_sq, "heads")
    denom = groups * feat_width * lax.axis_size("heads")
    factor = lax.rsqrt(total_sq / denom + EPS)[:, None, None]
    return (wide * factor).astype(jnp.bfloat16)


def solution(mesh):
    in_specs = (
        P("seq", "heads", None),
        P("seq", "heads", None),
        P("seq", "heads", None),
        P("heads", "seq"),
        P(),
        P("heads"),
        P("heads", "seq", None),
        P("heads", "seq", None),
        P("heads", "seq", None),
    )
    out_specs = P("seq", "heads", None)
    return jax.shard_map(shards, mesh=mesh, in_specs=in_specs, out_specs=out_specs, check_vma=False)
```

profile of v0, /device:TPU:1, one launch (start us, length us, event | category | flops | bytes accessed | tf_op | source)
XLA Modules:
  0.0 902.9 jit_solution(9635621633632806919)
XLA Ops:
  6.5 1.5 copy.110
  8.1 1.5 copy.113
  9.7 0.7 all-gather.6.cloned.1.call-update
  10.5 1.3 dynamic_slice.3
  11.7 0.6 fusion.62
  12.4 9.1 %fusion.74 = (bf16[2048,1,512]{2,1,0:T(2,128)(2,1)S(1)}, bf16[2048,1,512]{2,1,0:T(2,128)(2,1)S(1)}) fusion(bf16[2048,2,512]{2,1,0:T(2,128)(2,1)} %param.10), kind=kLoop, calls=%fused_computation.122 | loop fusion | bytes 8388608 | tf_op jit(solution)/shard_map/slice | solution.py:36
  21.6 2.6 copy_bitcast_fusion.2
  24.2 7.1 fusion.73
  31.3 114.4 %all-gather.4.cloned.1.call-done = f32[2,512,512]{2,0,1:T(2,128)} async-done(((f32[2,16,512]{2,0,1:T(2,128)}), f32[2,512,512]{2,0,1:T(2,128)}) %all-gather.4.cloned.1.call-update) | async-done | bytes 2097168 | tf_op jit(solution)/shard_map/all_gather | solution.py:76
  145.7 1.9 copy.167
  147.6 153.0 %all-gather.8.cloned.1.call-done = f32[2,512,512]{2,0,1:T(2,128)} async-done(((f32[2,16,512]{2,0,1:T(2,128)}), f32[2,512,512]{2,0,1:T(2,128)}) %all-gather.8.cloned.1.call-update) | async-done | bytes 2097168 | tf_op jit(solution)/shard_map/all_gather | solution.py:77
  300.5 1.9 copy.168
  302.4 3.2 fusion.60
  305.6 3.2 fusion.61
  308.8 3.3 fusion.58
  312.1 3.2 fusion.59
  315.4 140.1 %all-gather.6.cloned.1.call-done = f32[2,512,512]{2,1,0:T(8,128)} async-done(((f32[2,16,512]{2,1,0:T(8,128)}), f32[2,512,512]{2,1,0:T(8,128)}) %all-gather.6.cloned.1.call-update) | async-done | bytes 2097168 | tf_op jit(solution)/shard_map/all_gather | solution.py:78
  455.5 1.9 convert_element_type.111
  457.4 3.6 fusion.26
  461.1 4.4 fusion.40
  465.4 2.4 fusion.38
  467.9 1.3 fusion.46
  469.2 0.8 copy-done.13
  470.0 1.3 fusion.30
  471.3 1.4 copy-done.9
  472.7 2.2 fusion.43
  474.9 2.4 fusion.39
  477.3 1.3 fusion.47
  478.6 1.5 pad_maximum_fusion.1
  480.1 1.5 pad_maximum_fusion.3
  481.6 1.6 pad_maximum_fusion.2
  483.2 10.3 %fusion.72 = (bf16[2048,1,512]{2,1,0:T(2,128)(2,1)}, bf16[2048,1,512]{2,1,0:T(2,128)(2,1)}) fusion(bf16[2048,2,512]{2,1,0:T(2,128)(2,1)} %param.9), kind=kLoop, calls=%fused_computation.120 | loop fusion | bytes 8388608 | tf_op jit(solution)/shard_map/slice | solution.py:54
  493.5 0.9 multiply_reduce_fusion.4
  494.5 0.9 multiply_reduce_fusion.6
  495.5 4.2 copy.122
  499.7 3.0 copy.118
  502.7 323.1 %all-reduce.3.cloned.1.call-done = (f32[2,512,512]{1,2,0:T(8,128)}, f32[2,512,512]{2,1,0:T(8,128)}, f32[2,512,512]{1,2,0:T(8,128)}) async-done(((f32[2,512,512]{1,2,0:T(8,128)}, f32[2,512,512]{2,1,0:T(8,128)}, f32[2,512,512]{1,2,0:T(8,128)}), (f32[2,512,512]{1,2,0:T(8,128)}, f32[2,512,512]{2,1,0:T(8,128)}, f32[2,512,512]{1,2,0:T(8,128)})) %all-reduce.3.cloned.1.call-update) | async-done | bytes 6291472 | tf_op jit(solution)/shard_map/psum | solution.py:85
  825.8 2.9 multiply_reduce_fusion.5
  829.3 3.3 fusion.48
  832.5 3.3 fusion.49
  836.7 0.7 copy-done.7
  838.5 1.3 multiply_convert_fusion.11
  839.7 6.2 fusion.17
  846.0 7.5 fusion.19
  853.5 2.6 multiply_reduce_fusion
  856.2 24.6 %psum.31 = f32[2048]{0:T(1024)S(1)} all-reduce(f32[2048]{0:T(1024)S(1)} %multiply_reduce_fusion), channel_id=1, replica_groups=mesh['heads'=4,'seq'=32] {'heads'}, use_global_device_ids=true, to_apply=%region_10.11 | all-reduce | flops 2048 | bytes 16384 | tf_op jit(solution)/shard_map/psum | solution.py:95
  880.8 3.9 multiply_convert_fusion
  884.8 11.1 %copy.128 = bf16[2048,2,512]{2,1,0:T(2,128)(2,1)} copy(bf16[2048,2,512]{0,2,1:T(8,128)(2,1)} %multiply_convert_fusion) | data formatting | bytes 8388608 | tf_op jit(solution)/shard_map/convert_element_type | solution.py:98
  (52 shorter events, 3.0 us)
Async XLA Ops:
  6.5 139.1 %all-gather.4.cloned.1.call-start = ((), (), s32[]{:S(2)}) async-start(), calls=%async_computation | async-start | bytes 2162688 | tf_op jit(solution)/shard_map/all_gather | solution.py:76
  8.1 292.4 %all-gather.8.cloned.1.call-start = ((), (), s32[]{:S(2)}) async-start(), calls=%async_computation.2 | async-start | bytes 2162688 | tf_op jit(solution)/shard_map/all_gather | solution.py:77
  9.7 445.8 %all-gather.6.cloned.1.call-start = ((), (), s32[]{:S(2)}) async-start(), calls=%async_computation.1 | async-start | bytes 2162688 | tf_op jit(solution)/shard_map/all_gather | solution.py:78
  10.4 815.4 %all-reduce.3.cloned.1.call-start = ((), (), s32[]{:S(2)}) async-start(), calls=%async_computation.3 | async-start | bytes 12582912 | tf_op jit(solution)/shard_map/psum | solution.py:85
  12.4 9.2 %copy-start.16 = (bf16[2,2048]{1,0:T(2,128)(2,1)S(1)}, bf16[2,2048]{1,0:T(2,128)(2,1)}, u32[]{:S(2)}) copy-start(bf16[2,2048]{1,0:T(2,128)(2,1)} %param.12) | copy-start | bytes 24580
  21.6 2.6 copy-start.4
  305.6 3.2 copy-start
  455.5 5.5 copy-start.12
  457.4 3.7 copy-start.11
  461.1 4.4 copy-start.1
  467.8 2.2 copy-start.13
  467.8 3.5 copy-start.10
  469.2 3.5 copy-start.9
  483.2 10.3 %copy-start.3 = (f32[2,512,512]{2,0,1:T(2,128)S(1)}, f32[2,512,512]{2,0,1:T(2,128)}, u32[]{:S(2)}) copy-start(f32[2,512,512]{2,0,1:T(2,128)} %all-gather.8.cloned.1.call-done) | copy-start | bytes 6291460
  483.2 11.3 %copy-start.2 = (f32[2,512,512]{2,0,1:T(2,128)S(1)}, f32[2,512,512]{2,0,1:T(2,128)}, u32[]{:S(2)}) copy-start(f32[2,512,512]{2,0,1:T(2,128)} %all-gather.4.cloned.1.call-done) | copy-start | bytes 6291460
  825.8 3.4 copy-start.6
  829.0 3.5 copy-start.5
  832.5 3.3 copy-start.8
  832.5 3.3 copy-start.15
  835.8 1.6 copy-start.7
  835.8 2.2 copy-start.14
  846.0 7.6 copy-start.17
Sparse Core Ops, SparseCore 0:
  9.0 136.6 all-gather.3
  147.3 153.1 all-gather.7
  302.2 153.2 all-gather.5
  483.3 342.4 all-reduce.2
where the time goes:
time: 906 us; the launch traced here: 903 us
  waiting for transfers between devices  731 us (81%)
  local copies, waits for them, and re-layouts  59.6 us (7%)
  matrix products  52.1 us (6%)
  blocking collectives  24.6 us (3%)
  other arithmetic  21.3 us (2%)
  between operations  13.9 us (2%)
    psum x1, waiting for transfers between devices, shards(): summed = lax.psum((sums[0], sums[1], sums[2]), 'seq')  323 us
    all_gather x1, waiting for transfers between devices, shards(): lax.all_gather(w_third, 'seq', axis=1, tiled=True)  153 us
    all_gather x1, waiting for transfers between devices, shards(): lax.all_gather(w_second, 'seq', axis=1, tiled=True)  140 us
    all_gather x1, waiting for transfers between devices, shards(): lax.all_gather(w_first, 'seq', axis=1, tiled=True)  114 us
    psum x1, blocking collectives, shards(): total_sq = lax.psum(partial_sq, 'heads')  24.6 us
  transfers between devices with their start and end apart: 4, of which 4 were waited for; matrix products, arithmetic and copies ran while one was open for 6% of the time, Pallas kernels for 0%

commit v1 on v0

v1 whole, which is shorter than its diff:
```python
import functools
import jax
import jax.numpy as jnp
from jax import lax
from jax.experimental import pallas as pl
from jax.experimental.pallas import tpu as pltpu
from jax.sharding import PartitionSpec as P

EPS = 1e-06
VMEM_BYTES = 56 * 1024 * 1024
TERM_ROWS = 512
APPLY_ROWS = 512


def params():
    return pltpu.CompilerParams(vmem_limit_bytes=VMEM_BYTES)


def dot(a, b, dims):
    return lax.dot_general(a, b, (dims, ((), ())), preferred_element_type=jnp.float32)


def spread_kernel(w_first, w_third, w_second, wide):
    for mat, ref in enumerate((w_first, w_third, w_second)):
        part = ref[...].astype(jnp.bfloat16)
        for peer in range(wide.shape[0]):
            wide[peer, :, mat] = part


def spread(weights, peers):
    groups, rows, width = weights[0].shape
    return pl.pallas_call(
        spread_kernel,
        out_shape=jax.ShapeDtypeStruct((peers, groups, 3, rows, width), jnp.bfloat16),
        compiler_params=params(),
        name="spread",
    )(*weights)


def renew_kernel(blocks, w_first, w_third, w_second, wide):
    peers, groups = blocks.shape[:2]
    for mat, ref in enumerate((w_first, w_third, w_second)):
        for group in range(groups):
            term = jnp.sum(blocks[:, group, mat].astype(jnp.float32), axis=0)
            start = ref[group]
            update = start + term
            norm_old = jnp.mean(start * start, axis=-1, keepdims=True) + EPS
            norm_new = jnp.mean(update * update, axis=-1, keepdims=True) + EPS
            fresh = (update * (jnp.sqrt(norm_old) / jnp.sqrt(norm_new))).astype(jnp.bfloat16)
            for peer in range(peers):
                wide[peer, group, mat] = fresh


def renew(blocks, weights):
    return pl.pallas_call(
        renew_kernel,
        out_shape=jax.ShapeDtypeStruct(blocks.shape, jnp.bfloat16),
        compiler_params=params(),
        name="renew",
    )(blocks, *weights)


def terms_kernel(steps, k_ref, e_ref, b_ref, out, acc_in, acc_out):
    step = pl.program_id(1)
    width = k_ref.shape[1]
    k_part, err = k_ref[...], e_ref[...]
    b_one, b_three, b_two = (b_ref[:, 0, mat].reshape(width, width) for mat in range(3))
    h_one = dot(k_part, b_one, ((1,), (0,)))
    h_three = dot(k_part, b_three, ((1,), (0,)))
    back = dot(err, b_two, ((1,), (1,)))
    sig = jax.nn.sigmoid(h_one)
    gate = h_one * sig
    act = (gate * h_three).astype(jnp.bfloat16)
    d_one = (back * h_three * (sig * (1.0 + h_one * (1.0 - sig)))).astype(jnp.bfloat16)
    d_three = (back * gate).astype(jnp.bfloat16)
    p_in = dot(k_part, jnp.concatenate((d_one, d_three), axis=1), ((0,), (0,)))
    p_out = dot(act, err, ((0,), (0,)))

    @pl.when(step == 0)
    def _():
        acc_in[...] = p_in
        acc_out[...] = p_out

    @pl.when(step > 0)
    def _():
        acc_in[...] += p_in
        acc_out[...] += p_out

    @pl.when(step == steps - 1)
    def _():
        block = out.shape[:1] + out.shape[3:]
        out[:, 0, 0] = acc_in[:, :width].astype(jnp.bfloat16).reshape(block)
        out[:, 0, 1] = acc_in[:, width:].astype(jnp.bfloat16).reshape(block)
        out[:, 0, 2] = acc_out[...].astype(jnp.bfloat16).reshape(block)


def terms(k_flat, e_flat, halves):
    cap_rows = k_flat.shape[0]
    peers, groups, mats, rows, width = halves.shape
    steps = cap_rows // TERM_ROWS
    tokens = pl.BlockSpec((TERM_ROWS, width), lambda g, t: (t, g))
    weights = pl.BlockSpec((peers, 1, mats, rows, width), lambda g, t: (0, g, 0, 0, 0))
    return pl.pallas_call(
        functools.partial(terms_kernel, steps),
        grid=(groups, steps),
        in_specs=[tokens, tokens, weights],
        out_specs=weights,
        out_shape=jax.ShapeDtypeStruct(halves.shape, jnp.bfloat16),
        scratch_shapes=[
            pltpu.VMEM((width, 2 * width), jnp.float32),
            pltpu.VMEM((width, width), jnp.float32),
        ],
        compiler_params=params(),
        name="terms",
    )(k_flat, e_flat, halves)


def apply_kernel(q_ref, c_ref, live_ref, scale_ref, o_ref, ssq_ref):
    groups = c_ref.shape[1]
    width = q_ref.shape[1] // groups
    tokens = q_ref.shape[0]
    first = pl.program_id(0) * tokens
    live = first + lax.broadcasted_iota(jnp.int32, (tokens, width), 0) < live_ref[0]
    squares = jnp.zeros((tokens, 128), jnp.float32)
    for group in range(groups):
        q_part = q_ref[:, group * width : (group + 1) * width]
        c_one, c_three, c_two = (c_ref[:, group, mat].reshape(width, width) for mat in range(3))
        q_one = dot(q_part, c_one, ((1,), (0,)))
        q_three = dot(q_part, c_three, ((1,), (0,)))
        a_query = (q_one * jax.nn.sigmoid(q_one) * q_three).astype(jnp.bfloat16)
        o_part = dot(a_query, c_two, ((1,), (0,)))
        o_part = jnp.where(live, o_part, 0.0).astype(jnp.bfloat16)
        o_ref[:, group * width : (group + 1) * width] = o_part
        scaled = o_part.astype(jnp.float32) * scale_ref[group]
        scaled = scaled * scaled
        for col in range(width // 128):
            squares = squares + scaled[:, col * 128 : (col + 1) * 128]
    ssq_ref[...] = jnp.sum(squares.T, axis=0, keepdims=True)


def apply(q_flat, fresh, own_count, scales):
    cap_rows, both = q_flat.shape
    steps = cap_rows // APPLY_ROWS
    tokens = pl.BlockSpec((APPLY_ROWS, both), lambda t: (t, 0))
    return pl.pallas_call(
        apply_kernel,
        grid=(steps,),
        in_specs=[
            tokens,
            pl.BlockSpec(fresh.shape, lambda t: (0, 0, 0, 0, 0)),
            pl.BlockSpec(memory_space=pltpu.SMEM),
            pl.BlockSpec(memory_space=pltpu.SMEM),
        ],
        out_specs=[tokens, pl.BlockSpec((1, APPLY_ROWS), lambda t: (0, t))],
        out_shape=[
            jax.ShapeDtypeStruct(q_flat.shape, jnp.bfloat16),
            jax.ShapeDtypeStruct((1, cap_rows), jnp.float32),
        ],
        compiler_params=params(),
        name="apply",
    )(q_flat, fresh, own_count, scales)


def exchange(blocks):
    return lax.all_to_all(blocks, "seq", 0, 0, tiled=True)


def shards(
    queries, key_rows, value_rows, step_rates, live_counts, group_scales, w_first, w_third, w_second
):
    cap_rows, groups, feat_width = queries.shape
    seq_size = lax.axis_size("seq")
    root_total = jnp.sqrt(jnp.float32(cap_rows * seq_size))
    own_count = live_counts[lax.axis_index("seq")]
    live_mask = jnp.arange(cap_rows, dtype=jnp.int32) < own_count
    weights = (w_first, w_third, w_second)
    halves = exchange(spread(weights, seq_size))
    eta = step_rates.T.astype(jnp.float32) * live_mask.astype(jnp.float32)[:, None] / root_total
    err = (eta[:, :, None] * value_rows.astype(jnp.float32)).astype(jnp.bfloat16)
    flat = (cap_rows, groups * feat_width)
    sums = exchange(terms(key_rows.reshape(flat), err.reshape(flat), halves))
    fresh = exchange(renew(sums, weights))
    fast, partial_sq = apply(queries.reshape(flat), fresh, own_count[None], group_scales)
    total_sq = lax.psum(partial_sq[0], "heads")
    denom = groups * feat_width * lax.axis_size("heads")
    factor = lax.rsqrt(total_sq / denom + EPS)[:, None, None]
    wide = fast.reshape(queries.shape).astype(jnp.float32) * group_scales[None, :, None]
    return (wide * factor).astype(jnp.bfloat16)


def solution(mesh):
    in_specs = (
        P("seq", "heads", None),
        P("seq", "heads", None),
        P("seq", "heads", None),
        P("heads", "seq"),
        P(),
        P("heads"),
        P("heads", "seq", None),
        P("heads", "seq", None),
        P("heads", "seq", None),
    )
    out_specs = P("seq", "heads", None)
    return jax.shard_map(shards, mesh=mesh, in_specs=in_specs, out_specs=out_specs, check_vma=False)
```

time: 906 us -> 218 us (0.24)
  waiting for transfers between devices: 731 us -> 62.6 us
  matrix products: 52.1 us -> 0 us
  Pallas kernels: 0 us -> 41.8 us
  local copies, waits for them, and re-layouts: 59.6 us -> 28.6 us
  blocking collectives: 24.6 us -> 55.2 us
  starting transfers between devices: 0.12 us -> 14.4 us
  between operations: 13.9 us -> 0.11 us
    all_gather x3 -> x0, waiting for transfers between devices: 407 us -> none  [the longest x1 153 us: shards(): lax.all_gather(w_third, 'seq', axis=1, tiled=True)]
    psum x1 -> x0, waiting for transfers between devices: 323 us -> none  [shards(): summed = lax.psum((sums[0], sums[1], sums[2]), 'seq')]
    all_to_all x0 -> x2, waiting for transfers between devices: none -> 62.6 us  [exchange(): return lax.all_to_all(blocks, 'seq', 0, 0, tiled=True)]
    dot_general x16 -> x0, matrix products: 52.1 us -> none  [the longest x2 13.8 us: apply_rows(): jnp.dot(a_query, c_two[group], preferred_element_type=jnp.float32)]
    all_to_all x0 -> x1, blocking collectives: none -> 45.8 us  [exchange(): return lax.all_to_all(blocks, 'seq', 0, 0, tiled=True)]
    pallas_call x0 -> x4, Pallas kernels: none -> 41.8 us  [the longest x1 22.5 us: terms(): pl.pallas_call(functools.partial(terms_kernel, steps), grid=(groups, step...]
    slice x4 -> x0, local copies, waits for them, and re-layouts: 26.5 us -> none  [the longest x1 10.3 us: apply_rows(): q_part = q_rows[:, group]]
    psum x1, blocking collectives: 24.6 us -> 9.36 us  [shards(): total_sq = lax.psum(partial_sq[0], 'heads')]
  transfers between devices with their start and end apart: 4 -> 2, of which waited for: 4 -> 2; matrix products, arithmetic and copies ran while one was open for 6% -> 9% of each run, Pallas kernels for 0% -> 0%
where the time goes in v1:
time: 218 us; the launch traced here: 217 us
  waiting for transfers between devices  62.6 us (29%)
  blocking collectives  55.2 us (25%)
  Pallas kernels  41.8 us (19%)
  local copies, waits for them, and re-layouts  28.6 us (13%)
  starting transfers between devices  14.4 us (7%)
  other arithmetic  14.4 us (7%)
    all_to_all x2, waiting for transfers between devices, exchange(): return lax.all_to_all(blocks, 'seq', 0, 0, tiled=True)  62.6 us
    all_to_all x1, blocking collectives, exchange(): return lax.all_to_all(blocks, 'seq', 0, 0, tiled=True)  45.8 us
    pallas_call x1, Pallas kernels, terms(): pl.pallas_call(functools.partial(terms_kernel, steps), grid=(groups, step...  22.5 us
    unnamed x17, local copies, waits for them, and re-layouts  15.1 us
    all_to_all x2, starting transfers between devices, exchange(): return lax.all_to_all(blocks, 'seq', 0, 0, tiled=True)  14.4 us
    pallas_call x1, Pallas kernels, apply(): pl.pallas_call(apply_kernel, grid=(steps,), in_specs=[tokens, pl.BlockSpe...  12 us
    convert_element_type x1, local copies, waits for them, and re-layouts, shards(): fast.reshape(queries.shape).astype(jnp.float32)  11.6 us
    psum x1, blocking collectives, shards(): total_sq = lax.psum(partial_sq[0], 'heads')  9.36 us
  transfers between devices with their start and end apart: 2, of which 2 were waited for; matrix products, arithmetic and copies ran while one was open for 9% of the time, Pallas kernels for 0%

profile of v1, /device:TPU:1, one launch (start us, length us, event | category | flops | bytes accessed | tf_op | source)
XLA Modules:
  0.0 217.0 jit_solution(2393354849423115384)
XLA Ops:
  0.0 0.0 copy-start.6
  0.0 0.0 copy-start.4
  0.0 2.9 %spread.1 = bf16[32,2,3,16,512]{4,3,2,1,0:T(8,128)(2,1)} custom-call(f32[2,16,512]{2,1,0:T(8,128)} %w_first.3, f32[2,16,512]{2,1,0:T(8,128)} %w_third.3, f32[2,16,512]{2,1,0:T(8,128)} %w_second.3), custom_call_target="tpu_custom_call" | custom-call | tf_op jit(solution)/shard_map/spread/pallas_call | solution.py:32
  3.0 9.7 %all-to-all-start = ((bf16[32,2,3,16,512]{4,3,2,1,0:T(8,128)(2,1)}), bf16[32,2,3,16,512]{4,3,2,1,0:T(8,128)(2,1)S(1)}, u32[]{:S(2)}, u32[]{:S(2)}) async-start(bf16[32,2,3,16,512]{4,3,2,1,0:T(8,128)(2,1)} %spread.1), calls=%async_computation | async-start | bytes 6291456 | tf_op jit(solution)/shard_map/all_to_all | solution.py:165
  12.7 0.0 copy-done.6
  12.7 0.6 dynamic_slice.3.live_ref
  13.3 0.6 fusion
  13.8 0.0 copy-done.4
  13.9 1.3 copy.10
  15.2 5.4 %multiply_convert_fusion.1 = bf16[2048,2,512]{2,1,0:T(2,128)(2,1)S(1)} fusion(bf16[2048,2,512]{2,1,0:T(2,128)(2,1)} %param.11, f32[2048,2]{1,0:T(8,128)} %copy.10), kind=kLoop, calls=%fused_computation.1 | loop fusion | flops 6291456 | bytes 8404992 | tf_op jit(solution)/shard_map/convert_element_type | solution.py:179
  20.6 0.0 copy-start.2
  20.6 3.2 %copy.13 = bf16[256,8,2,512]{3,1,2,0:T(8,128)(2,1)} copy(bf16[256,8,2,512]{3,2,1,0:T(2,128)(2,1)S(1)} %bitcast.13) | data formatting | bytes 8388608
  23.7 0.0 copy-done.2
  23.7 3.2 %copy.12 = bf16[256,8,2,512]{3,1,2,0:T(8,128)(2,1)} copy(bf16[256,8,2,512]{3,2,1,0:T(2,128)(2,1)S(1)} %bitcast.14) | data formatting | bytes 8388608
  26.9 26.8 %all-to-all-done.b_ref = bf16[32,2,3,16,512]{4,3,2,1,0:T(8,128)(2,1)S(1)} async-done(((bf16[32,2,3,16,512]{4,3,2,1,0:T(8,128)(2,1)}), bf16[32,2,3,16,512]{4,3,2,1,0:T(8,128)(2,1)S(1)}, u32[]{:S(2)}, u32[]{:S(2)}) %all-to-all-start) | async-done | bytes 3145760 | tf_op jit(solution)/shard_map/all_to_all | solution.py:165
  53.8 0.0 copy-start
  53.8 1.7 copy-done
  55.5 22.5 %terms.1 = bf16[32,2,3,16,512]{4,3,2,1,0:T(8,128)(2,1)} custom-call(bf16[2048,1024]{1,0:T(8,128)(2,1)} %bitcast.11, bf16[2048,1024]{1,0:T(8,128)(2,1)} %bitcast.10, bf16[32,2,3,16,512]{4,3,2,1,0:T(8,128)(2,1)} %copy-done), custom_call_target="tpu_custom_call" | custom-call | tf_op jit(solution)/shard_map/terms/pallas_call | solution.py:103
  78.0 45.8 %all_to_all.15.blocks = bf16[32,2,3,16,512]{4,3,2,1,0:T(8,128)(2,1)} all-to-all(bf16[32,2,3,16,512]{4,3,2,1,0:T(8,128)(2,1)} %terms.1), channel_id=1, replica_groups=mesh['heads'=4,'seq'=32] {'seq'}, dimensions={0} | all-to-all | bytes 6291456 | tf_op jit(solution)/shard_map/all_to_all | solution.py:165
  123.8 4.3 %renew.1 = bf16[32,2,3,16,512]{4,3,2,1,0:T(8,128)(2,1)} custom-call(bf16[32,2,3,16,512]{4,3,2,1,0:T(8,128)(2,1)} %all_to_all.15.blocks, f32[2,16,512]{2,1,0:T(8,128)} %w_first.3, f32[2,16,512]{2,1,0:T(8,128)} %w_third.3, f32[2,16,512]{2,1,0:T(8,128)} %w_second.3), custom_call_target="tpu_custom_call" | custom-call | tf_op jit(solution)/shard_map/renew/pallas_call | solution.py:55
  128.1 4.6 %all-to-all-start.2 = ((bf16[32,2,3,16,512]{4,3,2,1,0:T(8,128)(2,1)}), bf16[32,2,3,16,512]{4,3,2,1,0:T(8,128)(2,1)S(1)}, u32[]{:S(2)}, u32[]{:S(2)}) async-start(bf16[32,2,3,16,512]{4,3,2,1,0:T(8,128)(2,1)} %renew.1), calls=%async_computation.2 | async-start | bytes 6291456 | tf_op jit(solution)/shard_map/all_to_all | solution.py:165
  132.7 5.4 %copy.11 = bf16[256,8,2,512]{3,1,2,0:T(8,128)(2,1)} copy(bf16[256,8,2,512]{3,2,1,0:T(2,128)(2,1)} %bitcast.15) | data formatting | bytes 8388608
  138.1 35.7 %all-to-all-done.2.c_ref = bf16[32,2,3,16,512]{4,3,2,1,0:T(8,128)(2,1)S(1)} async-done(((bf16[32,2,3,16,512]{4,3,2,1,0:T(8,128)(2,1)}), bf16[32,2,3,16,512]{4,3,2,1,0:T(8,128)(2,1)S(1)}, u32[]{:S(2)}, u32[]{:S(2)}) %all-to-all-start.2) | async-done | bytes 3145760 | tf_op jit(solution)/shard_map/all_to_all | solution.py:165
  173.9 0.0 copy-start.1
  173.9 1.6 copy-done.1
  175.5 12.0 %apply.1 = (bf16[2048,1024]{1,0:T(8,128)(2,1)}, f32[1,2048]{1,0:T(1,128)}) custom-call(bf16[2048,1024]{1,0:T(8,128)(2,1)} %bitcast.12, bf16[32,2,3,16,512]{4,3,2,1,0:T(8,128)(2,1)} %copy-done.1, s32[1]{0:T(128)} %dynamic_slice.3.live_ref, f32[2]{0:T(128)} %scale_ref.1), custom_call_target="tpu_custom_call" | custom-call | tf_op jit(solution)/shard_map/apply/pallas_call | solution.py:145
  187.5 0.0 copy-start.3
  187.6 0.0 copy-start.5
  187.6 11.6 %reshape.23 = f32[2048,2,512]{2,1,0:T(2,128)} reshape(bf16[2048,1024]{1,0:T(8,128)(2,1)} %get-tuple-element.7) | data formatting | bytes 12582912 | tf_op jit(solution)/shard_map/convert_element_type | solution.py:187
  199.1 0.0 copy-done.3
  199.1 9.4 %psum.7 = f32[2048]{0:T(1024)S(1)} all-reduce(f32[2048]{0:T(1024)S(1)} %bitcast.16), channel_id=1, replica_groups=mesh['heads'=4,'seq'=32] {'heads'}, use_global_device_ids=true, to_apply=%region_0.0 | all-reduce | flops 2048 | bytes 16384 | tf_op jit(solution)/shard_map/psum | solution.py:184
  208.5 0.0 copy-done.5
  208.5 8.5 %multiply_convert_fusion = bf16[2048,2,512]{2,1,0:T(2,128)(2,1)} fusion(f32[2048,2,512]{2,1,0:T(2,128)} %reshape.23, f32[2]{0:T(128)S(1)} %copy-done.5, f32[2048]{0:T(1024)S(1)} %add_rsqrt_fusion), kind=kLoop, calls=%fused_computation | loop fusion | flops 6291456 | bytes 12591112 | tf_op jit(solution)/shard_map/convert_element_type | solution.py:188
  (2 shorter events, 0.0 us)
Async XLA Ops:
  0.0 12.7 %copy-start.6 = (s32[32]{0:T(128)S(1)}, s32[32]{0:T(128)}, u32[]{:S(2)}) copy-start(s32[32]{0:T(128)} %param.13) | copy-start | bytes 388
  0.0 13.8 %copy-start.4 = (bf16[2,2048]{1,0:T(2,128)(2,1)S(1)}, bf16[2,2048]{1,0:T(2,128)(2,1)}, u32[]{:S(2)}) copy-start(bf16[2,2048]{1,0:T(2,128)(2,1)} %param.12) | copy-start | bytes 24580
  3.0 50.8 %all-to-all-start = ((bf16[32,2,3,16,512]{4,3,2,1,0:T(8,128)(2,1)}), bf16[32,2,3,16,512]{4,3,2,1,0:T(8,128)(2,1)S(1)}, u32[]{:S(2)}, u32[]{:S(2)}) async-start(bf16[32,2,3,16,512]{4,3,2,1,0:T(8,128)(2,1)} %spread.1), calls=%async_computation | async-start | bytes 6291456 | tf_op jit(solution)/shard_map/all_to_all | solution.py:165
  20.6 3.2 %copy-start.2 = (bf16[2048,2,512]{2,1,0:T(2,128)(2,1)S(1)}, bf16[2048,2,512]{2,1,0:T(2,128)(2,1)}, u32[]{:S(2)}) copy-start(bf16[2048,2,512]{2,1,0:T(2,128)(2,1)} %param.10) | copy-start | bytes 12582916
  53.8 1.7 copy-start
  128.1 45.8 %all-to-all-start.2 = ((bf16[32,2,3,16,512]{4,3,2,1,0:T(8,128)(2,1)}), bf16[32,2,3,16,512]{4,3,2,1,0:T(8,128)(2,1)S(1)}, u32[]{:S(2)}, u32[]{:S(2)}) async-start(bf16[32,2,3,16,512]{4,3,2,1,0:T(8,128)(2,1)} %renew.1), calls=%async_computation.2 | async-start | bytes 6291456 | tf_op jit(solution)/shard_map/all_to_all | solution.py:165
  173.9 1.6 copy-start.1
  187.5 11.6 %copy-start.3 = (f32[1,2048]{1,0:T(1,128)S(1)}, f32[1,2048]{1,0:T(1,128)}, u32[]{:S(2)}) copy-start(f32[1,2048]{1,0:T(1,128)} %get-tuple-element.8) | copy-start | bytes 24580
  187.6 20.9 %copy-start.5 = (f32[2]{0:T(128)S(1)}, f32[2]{0:T(128)}, u32[]{:S(2)}) copy-start(f32[2]{0:T(128)} %scale_ref.1) | copy-start | bytes 28

commit v2 on v1

--- a/solution.py
+++ b/solution.py
@@ -7,13 +7,13 @@
 from jax.sharding import PartitionSpec as P
 
 EPS = 1e-06
-VMEM_BYTES = 56 * 1024 * 1024
-TERM_ROWS = 512
+TERM_ROWS = 2048
 APPLY_ROWS = 512
-
-
-def params():
-    return pltpu.CompilerParams(vmem_limit_bytes=VMEM_BYTES)
+FINISH_ROWS = 512
+
+
+def params(mebibytes):
+    return pltpu.CompilerParams(vmem_limit_bytes=mebibytes * 1024 * 1024)
 
 
 def dot(a, b, dims):
@@ -32,7 +32,7 @@
     return pl.pallas_call(
         spread_kernel,
         out_shape=jax.ShapeDtypeStruct((peers, groups, 3, rows, width), jnp.bfloat16),
-        compiler_params=params(),
+        compiler_params=params(16),
         name="spread",
     )(*weights)
 
@@ -55,16 +55,16 @@
     return pl.pallas_call(
         renew_kernel,
         out_shape=jax.ShapeDtypeStruct(blocks.shape, jnp.bfloat16),
-        compiler_params=params(),
+        compiler_params=params(24),
         name="renew",
     )(blocks, *weights)
 
 
 def terms_kernel(steps, k_ref, e_ref, b_ref, out, acc_in, acc_out):
-    step = pl.program_id(1)
+    group, step = pl.program_id(0), pl.program_id(1)
     width = k_ref.shape[1]
     k_part, err = k_ref[...], e_ref[...]
-    b_one, b_three, b_two = (b_ref[:, 0, mat].reshape(width, width) for mat in range(3))
+    b_one, b_three, b_two = (b_ref[:, group, mat].reshape(width, width) for mat in range(3))
     h_one = dot(k_part, b_one, ((1,), (0,)))
     h_three = dot(k_part, b_three, ((1,), (0,)))
     back = dot(err, b_two, ((1,), (1,)))
@@ -103,14 +103,14 @@
     return pl.pallas_call(
         functools.partial(terms_kernel, steps),
         grid=(groups, steps),
-        in_specs=[tokens, tokens, weights],
+        in_specs=[tokens, tokens, pl.BlockSpec(memory_space=pltpu.VMEM)],
         out_specs=weights,
         out_shape=jax.ShapeDtypeStruct(halves.shape, jnp.bfloat16),
         scratch_shapes=[
             pltpu.VMEM((width, 2 * width), jnp.float32),
             pltpu.VMEM((width, width), jnp.float32),
         ],
-        compiler_params=params(),
+        compiler_params=params(40),
         name="terms",
     )(k_flat, e_flat, halves)
 
@@ -147,7 +147,7 @@
         grid=(steps,),
         in_specs=[
             tokens,
-            pl.BlockSpec(fresh.shape, lambda t: (0, 0, 0, 0, 0)),
+            pl.BlockSpec(memory_space=pltpu.VMEM),
             pl.BlockSpec(memory_space=pltpu.SMEM),
             pl.BlockSpec(memory_space=pltpu.SMEM),
         ],
@@ -156,9 +156,57 @@
             jax.ShapeDtypeStruct(q_flat.shape, jnp.bfloat16),
             jax.ShapeDtypeStruct((1, cap_rows), jnp.float32),
         ],
-        compiler_params=params(),
+        compiler_params=params(24),
         name="apply",
     )(q_flat, fresh, own_count, scales)
+
+
+def finish_kernel(o_ref, ssq_ref, scale_ref, out):
+    tokens, both = o_ref.shape
+    groups = scale_ref.shape[0]
+    width = both // groups
+    lanes = 128
+    tiles = width // lanes
+    side = 256
+    span = side // (groups * tiles)
+    factor = lax.rsqrt(ssq_ref[...] * scale_ref[groups - 1, 1] + EPS)
+    factor = jnp.broadcast_to(factor, (lanes, tokens)).T
+    columns = []
+    for start in range(0, tokens, span):
+        rows = slice(start, start + span)
+        pieces = []
+        for group in range(groups):
+            for tile in range(tiles):
+                col = group * width + tile * lanes
+                part = o_ref[rows, col : col + lanes].astype(jnp.float32) * scale_ref[group, 0]
+                pieces.append(part * factor[rows])
+        columns.append(jnp.concatenate(pieces, axis=0).astype(jnp.bfloat16))
+    row = lax.broadcasted_iota(jnp.int32, (side, side), 0)
+    col = lax.broadcasted_iota(jnp.int32, (side, side), 1)
+    token, tile, group = row // (groups * tiles), row % (groups * tiles) // groups, row % groups
+    order = jnp.where(col == (group * tiles + tile) * span + token, 1.0, 0.0).astype(jnp.bfloat16)
+    mixed = dot(order, jnp.concatenate(columns, axis=1), ((1,), (0,))).astype(jnp.bfloat16)
+    for index in range(len(columns)):
+        out[index * side : (index + 1) * side] = mixed[:, index * lanes : (index + 1) * lanes]
+
+
+def finish(fast, total_sq, scales):
+    cap_rows, both = fast.shape
+    lanes = 128
+    rows = FINISH_ROWS * both // lanes
+    return pl.pallas_call(
+        finish_kernel,
+        grid=(cap_rows // FINISH_ROWS,),
+        in_specs=[
+            pl.BlockSpec((FINISH_ROWS, both), lambda t: (t, 0)),
+            pl.BlockSpec((1, FINISH_ROWS), lambda t: (0, t)),
+            pl.BlockSpec(memory_space=pltpu.SMEM),
+        ],
+        out_specs=pl.BlockSpec((rows, lanes), lambda t: (t, 0)),
+        out_shape=jax.ShapeDtypeStruct((cap_rows * both // lanes, lanes), jnp.bfloat16),
+        compiler_params=params(16),
+        name="finish",
+    )(fast, total_sq, scales)
 
 
 def exchange(blocks):
@@ -181,11 +229,11 @@
     sums = exchange(terms(key_rows.reshape(flat), err.reshape(flat), halves))
     fresh = exchange(renew(sums, weights))
     fast, partial_sq = apply(queries.reshape(flat), fresh, own_count[None], group_scales)
-    total_sq = lax.psum(partial_sq[0], "heads")
-    denom = groups * feat_width * lax.axis_size("heads")
-    factor = lax.rsqrt(total_sq / denom + EPS)[:, None, None]
-    wide = fast.reshape(queries.shape).astype(jnp.float32) * group_scales[None, :, None]
-    return (wide * factor).astype(jnp.bfloat16)
+    total_sq = lax.psum(partial_sq, "heads")
+    share = jnp.full_like(group_scales, 1.0 / (groups * feat_width * lax.axis_size("heads")))
+    ordered = finish(fast, total_sq, jnp.stack((group_scales, share), axis=1))
+    ordered = ordered.reshape(cap_rows, feat_width // 128, groups, 128).transpose(0, 2, 1, 3)
+    return ordered.reshape(queries.shape)
 
 
 def solution(mesh):

time: 218 us -> 200 us (0.917)
  other arithmetic: 14.4 us -> 6 us
  Pallas kernels: 41.8 us -> 34.6 us
    convert_element_type x1 -> x0, local copies, waits for them, and re-layouts: 11.6 us -> none  [shards(): fast.reshape(queries.shape).astype(jnp.float32)]
    unnamed x17 -> x33, local copies, waits for them, and re-layouts: 15.1 us -> 24.6 us
    convert_element_type x1 -> x0, other arithmetic: 8.48 us -> none  [shards(): return (wide * factor).astype(jnp.bfloat16)]
    pallas_call x0 -> x1, Pallas kernels: none -> 4.29 us  [finish(): pl.pallas_call(finish_kernel, grid=(cap_rows // FINISH_ROWS,), in_specs=[...]
    pallas_call x1, Pallas kernels: 22.5 us -> 18.2 us  [terms(): pl.pallas_call(functools.partial(terms_kernel, steps), grid=(groups, step...]
    pallas_call x1, Pallas kernels: 12 us -> 9.44 us  [apply(): pl.pallas_call(apply_kernel, grid=(steps,), in_specs=[tokens, pl.BlockSpe...]
    pallas_call x1, Pallas kernels: 2.95 us -> 0.35 us  [spread(): pl.pallas_call(spread_kernel, out_shape=jax.ShapeDtypeStruct((peers, grou...]
  transfers between devices with their start and end apart: 2 -> 2, of which waited for: 2 -> 2; matrix products, arithmetic and copies ran while one was open for 9% -> 10% of each run, Pallas kernels for 0% -> 0%
where the time goes in v2:
time: 200 us; the launch traced here: 199 us
  waiting for transfers between devices  62.4 us (31%)
  blocking collectives  55 us (28%)
  Pallas kernels  34.6 us (17%)
  local copies, waits for them, and re-layouts  26.6 us (13%)
  starting transfers between devices  14.2 us (7%)
  other arithmetic  6 us (3%)
    all_to_all x2, waiting for transfers between devices, exchange(): return lax.all_to_all(blocks, 'seq', 0, 0, tiled=True)  62.4 us
    all_to_all x1, blocking collectives, exchange(): return lax.all_to_all(blocks, 'seq', 0, 0, tiled=True)  45.6 us
    unnamed x33, local copies, waits for them, and re-layouts  24.6 us
    pallas_call x1, Pallas kernels, terms(): pl.pallas_call(functools.partial(terms_kernel, steps), grid=(groups, step...  18.2 us
    all_to_all x2, starting transfers between devices, exchange(): return lax.all_to_all(blocks, 'seq', 0, 0, tiled=True)  14.2 us
    pallas_call x1, Pallas kernels, apply(): pl.pallas_call(apply_kernel, grid=(steps,), in_specs=[tokens, pl.BlockSpe...  9.44 us
    psum x1, blocking collectives, shards(): total_sq = lax.psum(partial_sq, 'heads')  9.34 us
    convert_element_type x1, other arithmetic, shards(): (eta[:, :, None] * value_rows.astype(jnp.float32)).astype(jnp.bfloat16)  5.35 us
  transfers between devices with their start and end apart: 2, of which 2 were waited for; matrix products, arithmetic and copies ran while one was open for 10% of the time, Pallas kernels for 0%

profile of v2, /device:TPU:1, one launch (start us, length us, event | category | flops | bytes accessed | tf_op | source)
XLA Modules:
  0.0 199.0 jit_solution(8933258549615513829)
XLA Ops:
  0.0 0.0 copy-start.5
  0.0 0.8 copy-done.5
  0.8 0.0 copy-start.7
  0.8 0.8 copy-done.7
  1.7 0.0 copy-start.9
  1.7 0.8 copy-done.9
  2.5 0.0 copy-start.14
  2.5 0.0 copy-start.13
  2.5 0.3 spread.1
  2.9 0.0 copy-start.2
  2.9 1.7 copy-done.2
  4.6 9.7 %all-to-all-start = ((bf16[32,2,3,16,512]{4,3,2,1,0:T(8,128)(2,1)}), bf16[32,2,3,16,512]{4,3,2,1,0:T(8,128)(2,1)S(1)}, u32[]{:S(2)}, u32[]{:S(2)}) async-start(bf16[32,2,3,16,512]{4,3,2,1,0:T(8,128)(2,1)} %copy-done.2), calls=%async_computation | async-start | bytes 6291456 | tf_op jit(solution)/shard_map/all_to_all | solution.py:213
  14.3 0.0 copy-done.14
  14.3 0.6 dynamic_slice.3.live_ref
  14.9 0.6 fusion
  15.6 0.0 copy-done.13
  15.6 1.3 copy.10
  17.0 5.4 %multiply_convert_fusion = bf16[2048,2,512]{2,1,0:T(2,128)(2,1)S(1)} fusion(bf16[2048,2,512]{2,1,0:T(2,128)(2,1)} %param.11, f32[2048,2]{1,0:T(8,128)} %copy.10), kind=kLoop, calls=%fused_computation | loop fusion | flops 6291456 | bytes 8404992 | tf_op jit(solution)/shard_map/convert_element_type | solution.py:227
  22.3 0.0 copy-start.12
  22.3 3.2 %copy.15 = bf16[256,8,2,512]{3,1,2,0:T(8,128)(2,1)} copy(bf16[256,8,2,512]{3,2,1,0:T(2,128)(2,1)S(1)} %bitcast.19) | data formatting | bytes 8388608
  25.5 0.0 copy-done.12
  25.5 3.2 %copy.14 = bf16[256,8,2,512]{3,1,2,0:T(8,128)(2,1)} copy(bf16[256,8,2,512]{3,2,1,0:T(2,128)(2,1)S(1)} %bitcast.20) | data formatting | bytes 8388608
  28.7 26.7 %all-to-all-done.b_ref = bf16[32,2,3,16,512]{4,3,2,1,0:T(8,128)(2,1)S(1)} async-done(((bf16[32,2,3,16,512]{4,3,2,1,0:T(8,128)(2,1)}), bf16[32,2,3,16,512]{4,3,2,1,0:T(8,128)(2,1)S(1)}, u32[]{:S(2)}, u32[]{:S(2)}) %all-to-all-start) | async-done | bytes 3145760 | tf_op jit(solution)/shard_map/all_to_all | solution.py:213
  55.4 0.0 copy-start
  55.4 2.2 %copy-done = bf16[256,8,2,512]{3,1,2,0:T(8,128)(2,1)S(1)} copy-done((bf16[256,8,2,512]{3,1,2,0:T(8,128)(2,1)S(1)}, bf16[256,8,2,512]{3,1,2,0:T(8,128)(2,1)}, u32[]{:S(2)}) %copy-start) | copy-done | bytes 4194328
  57.6 18.2 %terms.1 = bf16[32,2,3,16,512]{4,3,2,1,0:T(8,128)(2,1)S(1)} custom-call(bf16[2048,1024]{1,0:T(8,128)(2,1)S(1)} %bitcast.15, bf16[2048,1024]{1,0:T(8,128)(2,1)} %bitcast.18, bf16[32,2,3,16,512]{4,3,2,1,0:T(8,128)(2,1)S(1)} %all-to-all-done.b_ref), custom_call_target="tpu_custom_call" | custom-call | tf_op jit(solution)/shard_map/terms/pallas_call | solution.py:103
  75.8 0.0 copy-start.6
  75.8 0.0 copy-start.8
  75.8 0.0 copy-start.10
  75.8 45.6 %all_to_all.15.blocks = bf16[32,2,3,16,512]{4,3,2,1,0:T(8,128)(2,1)S(1)} all-to-all(bf16[32,2,3,16,512]{4,3,2,1,0:T(8,128)(2,1)S(1)} %terms.1), channel_id=1, replica_groups=mesh['heads'=4,'seq'=32] {'seq'}, dimensions={0} | all-to-all | bytes 6291456 | tf_op jit(solution)/shard_map/all_to_all | solution.py:213
  121.5 0.0 copy-done.6
  121.5 0.0 copy-done.8
  121.5 0.0 copy-done.10
  121.5 2.3 %renew.1 = bf16[32,2,3,16,512]{4,3,2,1,0:T(8,128)(2,1)} custom-call(bf16[32,2,3,16,512]{4,3,2,1,0:T(8,128)(2,1)S(1)} %all_to_all.15.blocks, f32[2,16,512]{2,1,0:T(8,128)S(1)} %copy-done.6, f32[2,16,512]{2,1,0:T(8,128)S(1)} %copy-done.8, f32[2,16,512]{2,1,0:T(8,128)S(1)} %copy-done.10), custom_call_target="tpu_custom_call" | custom-call | tf_op jit(solution)/shard_map/renew/pallas_call | solution.py:55
  123.8 4.5 %all-to-all-start.2 = ((bf16[32,2,3,16,512]{4,3,2,1,0:T(8,128)(2,1)}), bf16[32,2,3,16,512]{4,3,2,1,0:T(8,128)(2,1)S(1)}, u32[]{:S(2)}, u32[]{:S(2)}) async-start(bf16[32,2,3,16,512]{4,3,2,1,0:T(8,128)(2,1)} %renew.1), calls=%async_computation.2 | async-start | bytes 6291456 | tf_op jit(solution)/shard_map/all_to_all | solution.py:213
  128.3 0.0 copy-start.11
  128.3 5.4 %copy.13 = bf16[256,8,2,512]{3,1,2,0:T(8,128)(2,1)} copy(bf16[256,8,2,512]{3,2,1,0:T(2,128)(2,1)} %bitcast.21) | data formatting | bytes 8388608
  133.7 0.0 copy-done.11
  133.7 0.1 copy.11
  133.8 35.7 %all-to-all-done.2.c_ref = bf16[32,2,3,16,512]{4,3,2,1,0:T(8,128)(2,1)S(1)} async-done(((bf16[32,2,3,16,512]{4,3,2,1,0:T(8,128)(2,1)}), bf16[32,2,3,16,512]{4,3,2,1,0:T(8,128)(2,1)S(1)}, u32[]{:S(2)}, u32[]{:S(2)}) %all-to-all-start.2) | async-done | bytes 3145760 | tf_op jit(solution)/shard_map/all_to_all | solution.py:213
  169.5 2.2 %copy-done.1 = bf16[256,8,2,512]{3,1,2,0:T(8,128)(2,1)S(1)} copy-done((bf16[256,8,2,512]{3,1,2,0:T(8,128)(2,1)S(1)}, bf16[256,8,2,512]{3,1,2,0:T(8,128)(2,1)}, u32[]{:S(2)}) %copy-start.1) | copy-done | bytes 4194328
  171.7 9.4 %apply.1 = (bf16[2048,1024]{1,0:T(8,128)(2,1)S(1)}, f32[1,2048]{1,0:T(1,128)S(1)}) custom-call(bf16[2048,1024]{1,0:T(8,128)(2,1)S(1)} %bitcast.16, bf16[32,2,3,16,512]{4,3,2,1,0:T(8,128)(2,1)S(1)} %all-to-all-done.2.c_ref, s32[1]{0:T(128)} %dynamic_slice.3.live_ref, f32[2]{0:T(128)S(1)} %copy-done.11), custom_call_target="tpu_custom_call" | custom-call | tf_op jit(solution)/shard_map/apply/pallas_call | solution.py:145
  181.1 0.0 copy-start.3
  181.1 2.0 %copy-done.3 = bf16[2048,1024]{1,0:T(8,128)(2,1)} copy-done((bf16[2048,1024]{1,0:T(8,128)(2,1)}, bf16[2048,1024]{1,0:T(8,128)(2,1)S(1)}, u32[]{:S(2)}) %copy-start.3) | copy-done | bytes 4194328
  183.1 9.3 %psum.7.ssq_ref = f32[1,2048]{1,0:T(1,128)S(1)} all-reduce(f32[1,2048]{1,0:T(1,128)S(1)} %get-tuple-element.8), channel_id=1, replica_groups=mesh['heads'=4,'seq'=32] {'heads'}, use_global_device_ids=true, to_apply=%region_0.0 | all-reduce | flops 2048 | bytes 16384 | tf_op jit(solution)/shard_map/psum | solution.py:232
  192.5 0.0 copy-start.4
  192.5 2.2 %copy-done.4 = bf16[2048,1024]{1,0:T(8,128)(2,1)S(1)} copy-done((bf16[2048,1024]{1,0:T(8,128)(2,1)S(1)}, bf16[2048,1024]{1,0:T(8,128)(2,1)}, u32[]{:S(2)}) %copy-start.4) | copy-done | bytes 4194328
  194.7 4.3 %finish.1 = bf16[16384,128]{1,0:T(8,128)(2,1)} custom-call(bf16[2048,1024]{1,0:T(8,128)(2,1)S(1)} %copy-done.4, f32[1,2048]{1,0:T(1,128)S(1)} %psum.7.ssq_ref, f32[2,2]{1,0:T(2,128)S(1)} %stack.7.scale_ref), custom_call_target="tpu_custom_call" | custom-call | tf_op jit(solution)/shard_map/finish/pallas_call | solution.py:197
  (3 shorter events, 0.0 us)
Async XLA Ops:
  0.0 0.8 copy-start.5
  0.8 0.8 copy-start.7
  1.7 0.8 copy-start.9
  2.5 11.8 %copy-start.14 = (s32[32]{0:T(128)S(1)}, s32[32]{0:T(128)}, u32[]{:S(2)}) copy-start(s32[32]{0:T(128)} %param.13) | copy-start | bytes 388
  2.5 13.1 %copy-start.13 = (bf16[2,2048]{1,0:T(2,128)(2,1)S(1)}, bf16[2,2048]{1,0:T(2,128)(2,1)}, u32[]{:S(2)}) copy-start(bf16[2,2048]{1,0:T(2,128)(2,1)} %param.12) | copy-start | bytes 24580
  2.9 1.7 copy-start.2
  4.6 50.8 %all-to-all-start = ((bf16[32,2,3,16,512]{4,3,2,1,0:T(8,128)(2,1)}), bf16[32,2,3,16,512]{4,3,2,1,0:T(8,128)(2,1)S(1)}, u32[]{:S(2)}, u32[]{:S(2)}) async-start(bf16[32,2,3,16,512]{4,3,2,1,0:T(8,128)(2,1)} %copy-done.2), calls=%async_computation | async-start | bytes 6291456 | tf_op jit(solution)/shard_map/all_to_all | solution.py:213
  22.3 3.2 %copy-start.12 = (bf16[2048,2,512]{2,1,0:T(2,128)(2,1)S(1)}, bf16[2048,2,512]{2,1,0:T(2,128)(2,1)}, u32[]{:S(2)}) copy-start(bf16[2048,2,512]{2,1,0:T(2,128)(2,1)} %param.10) | copy-start | bytes 12582916
  55.4 2.2 %copy-start = (bf16[256,8,2,512]{3,1,2,0:T(8,128)(2,1)S(1)}, bf16[256,8,2,512]{3,1,2,0:T(8,128)(2,1)}, u32[]{:S(2)}) copy-start(bf16[256,8,2,512]{3,1,2,0:T(8,128)(2,1)} %copy.14) | copy-start | bytes 12582916
  75.8 45.7 %copy-start.6 = (f32[2,16,512]{2,1,0:T(8,128)S(1)}, f32[2,16,512]{2,1,0:T(8,128)}, u32[]{:S(2)}) copy-start(f32[2,16,512]{2,1,0:T(8,128)} %w_first.3) | copy-start | bytes 196612
  75.8 45.7 %copy-start.8 = (f32[2,16,512]{2,1,0:T(8,128)S(1)}, f32[2,16,512]{2,1,0:T(8,128)}, u32[]{:S(2)}) copy-start(f32[2,16,512]{2,1,0:T(8,128)} %w_third.3) | copy-start | bytes 196612
  75.8 45.6 %copy-start.10 = (f32[2,16,512]{2,1,0:T(8,128)S(1)}, f32[2,16,512]{2,1,0:T(8,128)}, u32[]{:S(2)}) copy-start(f32[2,16,512]{2,1,0:T(8,128)} %w_second.3) | copy-start | bytes 196612
  123.8 45.7 %all-to-all-start.2 = ((bf16[32,2,3,16,512]{4,3,2,1,0:T(8,128)(2,1)}), bf16[32,2,3,16,512]{4,3,2,1,0:T(8,128)(2,1)S(1)}, u32[]{:S(2)}, u32[]{:S(2)}) async-start(bf16[32,2,3,16,512]{4,3,2,1,0:T(8,128)(2,1)} %renew.1), calls=%async_computation.2 | async-start | bytes 6291456 | tf_op jit(solution)/shard_map/all_to_all | solution.py:213
  128.3 5.4 %copy-start.11 = (f32[2]{0:T(128)S(1)}, f32[2]{0:T(128)}, u32[]{:S(2)}) copy-start(f32[2]{0:T(128)} %scale_ref.1) | copy-start | bytes 28
  169.5 2.2 %copy-start.1 = (bf16[256,8,2,512]{3,1,2,0:T(8,128)(2,1)S(1)}, bf16[256,8,2,512]{3,1,2,0:T(8,128)(2,1)}, u32[]{:S(2)}) copy-start(bf16[256,8,2,512]{3,1,2,0:T(8,128)(2,1)} %copy.13) | copy-start | bytes 12582916
  181.1 2.0 %copy-start.3 = (bf16[2048,1024]{1,0:T(8,128)(2,1)}, bf16[2048,1024]{1,0:T(8,128)(2,1)S(1)}, u32[]{:S(2)}) copy-start(bf16[2048,1024]{1,0:T(8,128)(2,1)S(1)} %get-tuple-element.7.o_ref) | copy-start | bytes 12582916
  192.5 2.2 %copy-start.4 = (bf16[2048,1024]{1,0:T(8,128)(2,1)S(1)}, bf16[2048,1024]{1,0:T(8,128)(2,1)}, u32[]{:S(2)}) copy-start(bf16[2048,1024]{1,0:T(8,128)(2,1)} %copy-done.3) | copy-start | bytes 12582916

commit v3 on v2

--- a/solution.py
+++ b/solution.py
@@ -7,7 +7,11 @@
 from jax.sharding import PartitionSpec as P
 
 EPS = 1e-06
-TERM_ROWS = 2048
+TERM_ROWS = 512
+SPREAD_MIB = 60
+TERMS_MIB = 46
+APPLY_MIB = 50
+FINISH_MIB = 58
 APPLY_ROWS = 512
 FINISH_ROWS = 512
 
@@ -20,25 +24,37 @@
     return lax.dot_general(a, b, (dims, ((), ())), preferred_element_type=jnp.float32)
 
 
-def spread_kernel(w_first, w_third, w_second, wide):
+def send_all(chunk, wide, sems):
+    copies = [pltpu.make_async_copy(chunk, wide.at[peer], sems.at[peer]) for peer in range(wide.shape[0])]
+    for copy in copies:
+        copy.start()
+    for copy in copies:
+        copy.wait()
+
+
+def spread_kernel(w_first, w_third, w_second, wide, chunk, sems):
     for mat, ref in enumerate((w_first, w_third, w_second)):
-        part = ref[...].astype(jnp.bfloat16)
-        for peer in range(wide.shape[0]):
-            wide[peer, :, mat] = part
+        chunk[:, mat] = ref[...].astype(jnp.bfloat16)
+    send_all(chunk, wide, sems)
 
 
 def spread(weights, peers):
     groups, rows, width = weights[0].shape
     return pl.pallas_call(
         spread_kernel,
+        out_specs=pl.BlockSpec(memory_space=pl.ANY),
         out_shape=jax.ShapeDtypeStruct((peers, groups, 3, rows, width), jnp.bfloat16),
-        compiler_params=params(16),
+        scratch_shapes=[
+            pltpu.VMEM((groups, 3, rows, width), jnp.bfloat16),
+            pltpu.SemaphoreType.DMA((peers,)),
+        ],
+        compiler_params=params(SPREAD_MIB),
         name="spread",
     )(*weights)
 
 
-def renew_kernel(blocks, w_first, w_third, w_second, wide):
-    peers, groups = blocks.shape[:2]
+def renew_kernel(blocks, w_first, w_third, w_second, wide, chunk, sems):
+    groups = blocks.shape[1]
     for mat, ref in enumerate((w_first, w_third, w_second)):
         for group in range(groups):
             term = jnp.sum(blocks[:, group, mat].astype(jnp.float32), axis=0)
@@ -46,71 +62,85 @@
             update = start + term
             norm_old = jnp.mean(start * start, axis=-1, keepdims=True) + EPS
             norm_new = jnp.mean(update * update, axis=-1, keepdims=True) + EPS
-            fresh = (update * (jnp.sqrt(norm_old) / jnp.sqrt(norm_new))).astype(jnp.bfloat16)
-            for peer in range(peers):
-                wide[peer, group, mat] = fresh
+            fresh = update * (jnp.sqrt(norm_old) / jnp.sqrt(norm_new))
+            chunk[group, mat] = fresh.astype(jnp.bfloat16)
+    send_all(chunk, wide, sems)
 
 
 def renew(blocks, weights):
     return pl.pallas_call(
         renew_kernel,
+        out_specs=pl.BlockSpec(memory_space=pl.ANY),
         out_shape=jax.ShapeDtypeStruct(blocks.shape, jnp.bfloat16),
+        scratch_shapes=[
+            pltpu.VMEM(blocks.shape[1:], jnp.bfloat16),
+            pltpu.SemaphoreType.DMA(blocks.shape[:1]),
+        ],
         compiler_params=params(24),
         name="renew",
     )(blocks, *weights)
 
 
-def terms_kernel(steps, k_ref, e_ref, b_ref, out, acc_in, acc_out):
-    group, step = pl.program_id(0), pl.program_id(1)
-    width = k_ref.shape[1]
-    k_part, err = k_ref[...], e_ref[...]
-    b_one, b_three, b_two = (b_ref[:, group, mat].reshape(width, width) for mat in range(3))
-    h_one = dot(k_part, b_one, ((1,), (0,)))
-    h_three = dot(k_part, b_three, ((1,), (0,)))
-    back = dot(err, b_two, ((1,), (1,)))
-    sig = jax.nn.sigmoid(h_one)
-    gate = h_one * sig
-    act = (gate * h_three).astype(jnp.bfloat16)
-    d_one = (back * h_three * (sig * (1.0 + h_one * (1.0 - sig)))).astype(jnp.bfloat16)
-    d_three = (back * gate).astype(jnp.bfloat16)
-    p_in = dot(k_part, jnp.concatenate((d_one, d_three), axis=1), ((0,), (0,)))
-    p_out = dot(act, err, ((0,), (0,)))
-
-    @pl.when(step == 0)
-    def _():
-        acc_in[...] = p_in
-        acc_out[...] = p_out
-
-    @pl.when(step > 0)
-    def _():
-        acc_in[...] += p_in
-        acc_out[...] += p_out
-
-    @pl.when(step == steps - 1)
-    def _():
-        block = out.shape[:1] + out.shape[3:]
-        out[:, 0, 0] = acc_in[:, :width].astype(jnp.bfloat16).reshape(block)
-        out[:, 0, 1] = acc_in[:, width:].astype(jnp.bfloat16).reshape(block)
-        out[:, 0, 2] = acc_out[...].astype(jnp.bfloat16).reshape(block)
+def terms_kernel(k_hbm, e_hbm, b_ref, out, k_ref, e_ref, d_ref, a_ref, k_sems, e_sems):
+    groups = b_ref.shape[1]
+    cap_rows = k_hbm.shape[0]
+    width = k_hbm.shape[1] // groups
+    block = out.shape[:1] + out.shape[3:]
+    copies = {}
+    for group in range(groups):
+        cols = pl.ds(group * width, width)
+        for part in range(cap_rows // TERM_ROWS):
+            rows = pl.ds(part * TERM_ROWS, TERM_ROWS)
+            copies[group, part] = (
+                pltpu.make_async_copy(k_hbm.at[rows, cols], k_ref.at[group, rows], k_sems.at[group, part]),
+                pltpu.make_async_copy(e_hbm.at[rows, cols], e_ref.at[group, rows], e_sems.at[group, part]),
+            )
+            for copy in copies[group, part]:
+                copy.start()
+    for group in range(groups):
+        b_one, b_three, b_two = (b_ref[:, group, mat].reshape(width, width) for mat in range(3))
+        for part in range(cap_rows // TERM_ROWS):
+            for copy in copies[group, part]:
+                copy.wait()
+            rows = slice(part * TERM_ROWS, (part + 1) * TERM_ROWS)
+            k_part, err = k_ref[group, rows], e_ref[group, rows]
+            h_one = dot(k_part, b_one, ((1,), (0,)))
+            h_three = dot(k_part, b_three, ((1,), (0,)))
+            back = dot(err, b_two, ((1,), (1,)))
+            sig = 0.5 * jnp.tanh(0.5 * h_one) + 0.5
+            gate = h_one * sig
+            a_ref[rows] = (gate * h_three).astype(jnp.bfloat16)
+            d_ref[rows, :width] = (back * h_three * (sig + gate * (1.0 - sig))).astype(jnp.bfloat16)
+            d_ref[rows, width:] = (back * gate).astype(jnp.bfloat16)
+        p_in = dot(k_ref[group], d_ref[...], ((0,), (0,)))
+        out[:, group, 0] = p_in[:, :width].astype(jnp.bfloat16).reshape(block)
+        out[:, group, 1] = p_in[:, width:].astype(jnp.bfloat16).reshape(block)
+        p_out = dot(a_ref[...], e_ref[group], ((0,), (0,)))
+        out[:, group, 2] = p_out.astype(jnp.bfloat16).reshape(block)
 
 
 def terms(k_flat, e_flat, halves):
     cap_rows = k_flat.shape[0]
-    peers, groups, mats, rows, width = halves.shape
-    steps = cap_rows // TERM_ROWS
-    tokens = pl.BlockSpec((TERM_ROWS, width), lambda g, t: (t, g))
-    weights = pl.BlockSpec((peers, 1, mats, rows, width), lambda g, t: (0, g, 0, 0, 0))
-    return pl.pallas_call(
-        functools.partial(terms_kernel, steps),
-        grid=(groups, steps),
-        in_specs=[tokens, tokens, pl.BlockSpec(memory_space=pltpu.VMEM)],
-        out_specs=weights,
+    groups, width = halves.shape[1], halves.shape[4]
+    parts = cap_rows // TERM_ROWS
+    return pl.pallas_call(
+        terms_kernel,
+        in_specs=[
+            pl.BlockSpec(memory_space=pl.ANY),
+            pl.BlockSpec(memory_space=pl.ANY),
+            pl.BlockSpec(memory_space=pltpu.VMEM),
+        ],
+        out_specs=pl.BlockSpec(memory_space=pltpu.VMEM),
         out_shape=jax.ShapeDtypeStruct(halves.shape, jnp.bfloat16),
         scratch_shapes=[
-            pltpu.VMEM((width, 2 * width), jnp.float32),
-            pltpu.VMEM((width, width), jnp.float32),
-        ],
-        compiler_params=params(40),
+            pltpu.VMEM((groups, cap_rows, width), jnp.bfloat16),
+            pltpu.VMEM((groups, cap_rows, width), jnp.bfloat16),
+            pltpu.VMEM((cap_rows, 2 * width), jnp.bfloat16),
+            pltpu.VMEM((cap_rows, width), jnp.bfloat16),
+            pltpu.SemaphoreType.DMA((groups, parts)),
+            pltpu.SemaphoreType.DMA((groups, parts)),
+        ],
+        compiler_params=params(TERMS_MIB),
         name="terms",
     )(k_flat, e_flat, halves)
 
@@ -127,7 +157,7 @@
         c_one, c_three, c_two = (c_ref[:, group, mat].reshape(width, width) for mat in range(3))
         q_one = dot(q_part, c_one, ((1,), (0,)))
         q_three = dot(q_part, c_three, ((1,), (0,)))
-        a_query = (q_one * jax.nn.sigmoid(q_one) * q_three).astype(jnp.bfloat16)
+        a_query = (q_one * (0.5 * jnp.tanh(0.5 * q_one) + 0.5) * q_three).astype(jnp.bfloat16)
         o_part = dot(a_query, c_two, ((1,), (0,)))
         o_part = jnp.where(live, o_part, 0.0).astype(jnp.bfloat16)
         o_ref[:, group * width : (group + 1) * width] = o_part
@@ -156,7 +186,7 @@
             jax.ShapeDtypeStruct(q_flat.shape, jnp.bfloat16),
             jax.ShapeDtypeStruct((1, cap_rows), jnp.float32),
         ],
-        compiler_params=params(24),
+        compiler_params=params(APPLY_MIB),
         name="apply",
     )(q_flat, fresh, own_count, scales)
 
@@ -169,7 +199,8 @@
     tiles = width // lanes
     side = 256
     span = side // (groups * tiles)
-    factor = lax.rsqrt(ssq_ref[...] * scale_ref[groups - 1, 1] + EPS)
+    total_sq = jnp.sum(ssq_ref[...], axis=0, keepdims=True)
+    factor = lax.rsqrt(total_sq * scale_ref[groups - 1, 1] + EPS)
     factor = jnp.broadcast_to(factor, (lanes, tokens)).T
     columns = []
     for start in range(0, tokens, span):
@@ -199,12 +230,12 @@
         grid=(cap_rows // FINISH_ROWS,),
         in_specs=[
             pl.BlockSpec((FINISH_ROWS, both), lambda t: (t, 0)),
-            pl.BlockSpec((1, FINISH_ROWS), lambda t: (0, t)),
+            pl.BlockSpec((total_sq.shape[0], FINISH_ROWS), lambda t: (0, t)),
             pl.BlockSpec(memory_space=pltpu.SMEM),
         ],
         out_specs=pl.BlockSpec((rows, lanes), lambda t: (t, 0)),
         out_shape=jax.ShapeDtypeStruct((cap_rows * both // lanes, lanes), jnp.bfloat16),
-        compiler_params=params(16),
+        compiler_params=params(FINISH_MIB),
         name="finish",
     )(fast, total_sq, scales)
 
@@ -229,7 +260,7 @@
     sums = exchange(terms(key_rows.reshape(flat), err.reshape(flat), halves))
     fresh = exchange(renew(sums, weights))
     fast, partial_sq = apply(queries.reshape(flat), fresh, own_count[None], group_scales)
-    total_sq = lax.psum(partial_sq, "heads")
+    total_sq = lax.all_gather(partial_sq, "heads", axis=0, tiled=True)
     share = jnp.full_like(group_scales, 1.0 / (groups * feat_width * lax.axis_size("heads")))
     ordered = finish(fast, total_sq, jnp.stack((group_scales, share), axis=1))
     ordered = ordered.reshape(cap_rows, feat_width // 128, groups, 128).transpose(0, 2, 1, 3)

time: 200 us -> 193 us (0.965)
  local copies, waits for them, and re-layouts: 26.6 us -> 15 us
  Pallas kernels: 34.6 us -> 40.2 us
    unnamed x33 -> x18, local copies, waits for them, and re-layouts: 24.6 us -> 12.4 us
    psum x1 -> x0, blocking collectives: 9.34 us -> none  [shards(): total_sq = lax.psum(partial_sq, 'heads')]
    all_gather x0 -> x1, blocking collectives: none -> 9.23 us  [shards(): total_sq = lax.all_gather(partial_sq, 'heads', axis=0, tiled=True)]
    pallas_call x3, Pallas kernels: 20.9 us -> 23.3 us  [the longest x1 18 us: terms(): pl.pallas_call(terms_kernel, in_specs=[pl.BlockSpec(memory_space=pl.ANY),...]
  transfers between devices with their start and end apart: 2 -> 2, of which waited for: 2 -> 2; matrix products, arithmetic and copies ran while one was open for 10% -> 11% of each run, Pallas kernels for 0% -> 0%
where the time goes in v3:
time: 193 us; the launch traced here: 192 us
  waiting for transfers between devices  62.1 us (32%)
  blocking collectives  54.9 us (28%)
  Pallas kernels  40.2 us (21%)
  local copies, waits for them, and re-layouts  15 us (8%)
  starting transfers between devices  14.2 us (7%)
  other arithmetic  5.91 us (3%)
    all_to_all x2, waiting for transfers between devices, exchange(): return lax.all_to_all(blocks, 'seq', 0, 0, tiled=True)  62.1 us
    all_to_all x1, blocking collectives, exchange(): return lax.all_to_all(blocks, 'seq', 0, 0, tiled=True)  45.6 us
    pallas_call x1, Pallas kernels, terms(): pl.pallas_call(terms_kernel, in_specs=[pl.BlockSpec(memory_space=pl.ANY),...  18 us
    all_to_all x2, starting transfers between devices, exchange(): return lax.all_to_all(blocks, 'seq', 0, 0, tiled=True)  14.2 us
    unnamed x18, local copies, waits for them, and re-layouts  12.4 us
    pallas_call x1, Pallas kernels, apply(): pl.pallas_call(apply_kernel, grid=(steps,), in_specs=[tokens, pl.BlockSpe...  11 us
    all_gather x1, blocking collectives, shards(): total_sq = lax.all_gather(partial_sq, 'heads', axis=0, tiled=True)  9.23 us
    pallas_call x1, Pallas kernels, finish(): pl.pallas_call(finish_kernel, grid=(cap_rows // FINISH_ROWS,), in_specs=[...  5.82 us
  transfers between devices with their start and end apart: 2, of which 2 were waited for; matrix products, arithmetic and copies ran while one was open for 11% of the time, Pallas kernels for 0%

profile of v3, /device:TPU:1, one launch (start us, length us, event | category | flops | bytes accessed | tf_op | source)
XLA Modules:
  0.0 192.3 jit_solution(2714834297895800125)
XLA Ops:
  0.0 0.0 copy-start.6
  0.0 0.0 copy-start.5
  0.0 2.9 %spread.1 = bf16[32,2,3,16,512]{4,3,2,1,0:T(8,128)(2,1)} custom-call(f32[2,16,512]{2,1,0:T(8,128)} %w_first.3, f32[2,16,512]{2,1,0:T(8,128)} %w_third.3, f32[2,16,512]{2,1,0:T(8,128)} %w_second.3), custom_call_target="tpu_custom_call" | custom-call | tf_op jit(solution)/shard_map/spread/pallas_call | solution.py:43
  2.9 9.7 %all-to-all-start = ((bf16[32,2,3,16,512]{4,3,2,1,0:T(8,128)(2,1)}), bf16[32,2,3,16,512]{4,3,2,1,0:T(8,128)(2,1)S(1)}, u32[]{:S(2)}, u32[]{:S(2)}) async-start(bf16[32,2,3,16,512]{4,3,2,1,0:T(8,128)(2,1)} %spread.1), calls=%async_computation | async-start | bytes 6291456 | tf_op jit(solution)/shard_map/all_to_all | solution.py:244
  12.7 0.0 copy-done.6
  12.7 0.6 dynamic_slice.3.live_ref
  13.2 0.5 fusion
  13.8 0.0 copy-done.5
  13.8 1.3 copy.13
  15.2 5.4 %multiply_convert_fusion = bf16[2048,2,512]{2,1,0:T(2,128)(2,1)S(1)} fusion(bf16[2048,2,512]{2,1,0:T(2,128)(2,1)} %param.11, f32[2048,2]{1,0:T(8,128)} %copy.13), kind=kLoop, calls=%fused_computation | loop fusion | flops 6291456 | bytes 8404992 | tf_op jit(solution)/shard_map/convert_element_type | solution.py:258
  20.5 0.0 copy-start.4
  20.5 3.2 %copy.19 = bf16[256,8,2,512]{3,1,2,0:T(8,128)(2,1)} copy(bf16[256,8,2,512]{3,2,1,0:T(2,128)(2,1)S(1)} %bitcast.24) | data formatting | bytes 8388608
  23.7 0.0 copy-done.4
  23.7 3.2 %copy.18 = bf16[256,8,2,512]{3,1,2,0:T(8,128)(2,1)} copy(bf16[256,8,2,512]{3,2,1,0:T(2,128)(2,1)S(1)} %bitcast.25) | data formatting | bytes 8388608
  26.9 26.8 %all-to-all-done.b_ref = bf16[32,2,3,16,512]{4,3,2,1,0:T(8,128)(2,1)S(1)} async-done(((bf16[32,2,3,16,512]{4,3,2,1,0:T(8,128)(2,1)}), bf16[32,2,3,16,512]{4,3,2,1,0:T(8,128)(2,1)S(1)}, u32[]{:S(2)}, u32[]{:S(2)}) %all-to-all-start) | async-done | bytes 3145760 | tf_op jit(solution)/shard_map/all_to_all | solution.py:244
  53.7 18.0 %terms.1 = bf16[32,2,3,16,512]{4,3,2,1,0:T(8,128)(2,1)S(1)} custom-call(bf16[2048,1024]{1,0:T(8,128)(2,1)} %bitcast.22, bf16[2048,1024]{1,0:T(8,128)(2,1)} %bitcast.21, bf16[32,2,3,16,512]{4,3,2,1,0:T(8,128)(2,1)S(1)} %all-to-all-done.b_ref), custom_call_target="tpu_custom_call" | custom-call | tf_op jit(solution)/shard_map/terms/pallas_call | solution.py:126
  71.7 0.0 copy-start
  71.7 0.0 copy-start.1
  71.7 0.0 copy-start.2
  71.7 45.6 %all_to_all.15.blocks = bf16[32,2,3,16,512]{4,3,2,1,0:T(8,128)(2,1)S(1)} all-to-all(bf16[32,2,3,16,512]{4,3,2,1,0:T(8,128)(2,1)S(1)} %terms.1), channel_id=1, replica_groups=mesh['heads'=4,'seq'=32] {'seq'}, dimensions={0} | all-to-all | bytes 6291456 | tf_op jit(solution)/shard_map/all_to_all | solution.py:244
  117.4 0.0 copy-done
  117.4 0.0 copy-done.1
  117.4 0.0 copy-done.2
  117.4 2.5 %renew.1 = bf16[32,2,3,16,512]{4,3,2,1,0:T(8,128)(2,1)} custom-call(bf16[32,2,3,16,512]{4,3,2,1,0:T(8,128)(2,1)S(1)} %all_to_all.15.blocks, f32[2,16,512]{2,1,0:T(8,128)S(1)} %copy-done, f32[2,16,512]{2,1,0:T(8,128)S(1)} %copy-done.1, f32[2,16,512]{2,1,0:T(8,128)S(1)} %copy-done.2), custom_call_target="tpu_custom_call" | custom-call | tf_op jit(solution)/shard_map/renew/pallas_call | solution.py:71
  119.9 4.5 %all-to-all-start.2 = ((bf16[32,2,3,16,512]{4,3,2,1,0:T(8,128)(2,1)}), bf16[32,2,3,16,512]{4,3,2,1,0:T(8,128)(2,1)S(1)}, u32[]{:S(2)}, u32[]{:S(2)}) async-start(bf16[32,2,3,16,512]{4,3,2,1,0:T(8,128)(2,1)} %renew.1), calls=%async_computation.2 | async-start | bytes 6291456 | tf_op jit(solution)/shard_map/all_to_all | solution.py:244
  124.4 0.0 copy-start.3
  124.4 5.4 %copy.17 = bf16[256,8,2,512]{3,1,2,0:T(8,128)(2,1)} copy(bf16[256,8,2,512]{3,2,1,0:T(2,128)(2,1)} %bitcast.26) | data formatting | bytes 8388608
  129.8 0.0 copy-done.3
  129.8 0.1 copy.14
  129.9 0.6 stack.7.scale_ref
  130.4 35.2 %all-to-all-done.2.c_ref = bf16[32,2,3,16,512]{4,3,2,1,0:T(8,128)(2,1)S(1)} async-done(((bf16[32,2,3,16,512]{4,3,2,1,0:T(8,128)(2,1)}), bf16[32,2,3,16,512]{4,3,2,1,0:T(8,128)(2,1)S(1)}, u32[]{:S(2)}, u32[]{:S(2)}) %all-to-all-start.2) | async-done | bytes 3145760 | tf_op jit(solution)/shard_map/all_to_all | solution.py:244
  165.7 11.0 %apply.1 = (bf16[2048,1024]{1,0:T(8,128)(2,1)}, f32[1,2048]{1,0:T(1,128)S(1)}) custom-call(bf16[2048,1024]{1,0:T(8,128)(2,1)} %bitcast.23, bf16[32,2,3,16,512]{4,3,2,1,0:T(8,128)(2,1)S(1)} %all-to-all-done.2.c_ref, s32[1]{0:T(128)} %dynamic_slice.3.live_ref, f32[2]{0:T(128)S(1)} %copy-done.3), custom_call_target="tpu_custom_call" | custom-call | tf_op jit(solution)/shard_map/apply/pallas_call | solution.py:175
  176.7 9.2 %all-gather = f32[4,1,2048]{2,1,0:T(1,128)S(1)} all-gather(f32[1,1,2048]{2,1,0:T(1,128)S(1)} %bitcast.19), channel_id=1, replica_groups=mesh['heads'=4,'seq'=32] {'heads'}, dimensions={0}, use_global_device_ids=true | all-gather | bytes 40960 | tf_op jit(solution)/shard_map/all_gather | solution.py:263
  185.9 0.6 copy.21
  186.5 5.8 %finish.1 = bf16[16384,128]{1,0:T(8,128)(2,1)} custom-call(bf16[2048,1024]{1,0:T(8,128)(2,1)} %get-tuple-element.7.o_ref, f32[4,2048]{1,0:T(4,128)} %bitcast.27, f32[2,2]{1,0:T(2,128)} %stack.7.scale_ref), custom_call_target="tpu_custom_call" | custom-call | tf_op jit(solution)/shard_map/finish/pallas_call | solution.py:228
  (1 shorter events, 0.0 us)
Async XLA Ops:
  0.0 12.7 %copy-start.6 = (s32[32]{0:T(128)S(1)}, s32[32]{0:T(128)}, u32[]{:S(2)}) copy-start(s32[32]{0:T(128)} %param.13) | copy-start | bytes 388
  0.0 13.8 %copy-start.5 = (bf16[2,2048]{1,0:T(2,128)(2,1)S(1)}, bf16[2,2048]{1,0:T(2,128)(2,1)}, u32[]{:S(2)}) copy-start(bf16[2,2048]{1,0:T(2,128)(2,1)} %param.12) | copy-start | bytes 24580
  2.9 50.8 %all-to-all-start = ((bf16[32,2,3,16,512]{4,3,2,1,0:T(8,128)(2,1)}), bf16[32,2,3,16,512]{4,3,2,1,0:T(8,128)(2,1)S(1)}, u32[]{:S(2)}, u32[]{:S(2)}) async-start(bf16[32,2,3,16,512]{4,3,2,1,0:T(8,128)(2,1)} %spread.1), calls=%async_computation | async-start | bytes 6291456 | tf_op jit(solution)/shard_map/all_to_all | solution.py:244
  20.5 3.2 %copy-start.4 = (bf16[2048,2,512]{2,1,0:T(2,128)(2,1)S(1)}, bf16[2048,2,512]{2,1,0:T(2,128)(2,1)}, u32[]{:S(2)}) copy-start(bf16[2048,2,512]{2,1,0:T(2,128)(2,1)} %param.10) | copy-start | bytes 12582916
  71.7 45.7 %copy-start = (f32[2,16,512]{2,1,0:T(8,128)S(1)}, f32[2,16,512]{2,1,0:T(8,128)}, u32[]{:S(2)}) copy-start(f32[2,16,512]{2,1,0:T(8,128)} %w_first.3) | copy-start | bytes 196612
  71.7 45.7 %copy-start.1 = (f32[2,16,512]{2,1,0:T(8,128)S(1)}, f32[2,16,512]{2,1,0:T(8,128)}, u32[]{:S(2)}) copy-start(f32[2,16,512]{2,1,0:T(8,128)} %w_third.3) | copy-start | bytes 196612
  71.7 45.6 %copy-start.2 = (f32[2,16,512]{2,1,0:T(8,128)S(1)}, f32[2,16,512]{2,1,0:T(8,128)}, u32[]{:S(2)}) copy-start(f32[2,16,512]{2,1,0:T(8,128)} %w_second.3) | copy-start | bytes 196612
  119.9 45.8 %all-to-all-start.2 = ((bf16[32,2,3,16,512]{4,3,2,1,0:T(8,128)(2,1)}), bf16[32,2,3,16,512]{4,3,2,1,0:T(8,128)(2,1)S(1)}, u32[]{:S(2)}, u32[]{:S(2)}) async-start(bf16[32,2,3,16,512]{4,3,2,1,0:T(8,128)(2,1)} %renew.1), calls=%async_computation.2 | async-start | bytes 6291456 | tf_op jit(solution)/shard_map/all_to_all | solution.py:244
  124.4 5.4 %copy-start.3 = (f32[2]{0:T(128)S(1)}, f32[2]{0:T(128)}, u32[]{:S(2)}) copy-start(f32[2]{0:T(128)} %scale_ref.1) | copy-start | bytes 28

commit v4 on v3

--- a/solution.py
+++ b/solution.py
@@ -13,7 +13,7 @@
 APPLY_MIB = 50
 FINISH_MIB = 58
 APPLY_ROWS = 512
-FINISH_ROWS = 512
+FINISH_ROWS = 1024
 
 
 def params(mebibytes):
@@ -79,6 +79,14 @@
         compiler_params=params(24),
         name="renew",
     )(blocks, *weights)
+
+
+def arrivals(group, part, parts):
+    if group == 0 and part == 0:
+        return [0]
+    if part == (1 if group == 0 else 0):
+        return range(part, parts)
+    return []
 
 
 def terms_kernel(k_hbm, e_hbm, b_ref, out, k_ref, e_ref, d_ref, a_ref, k_sems, e_sems):
@@ -100,15 +108,18 @@
     for group in range(groups):
         b_one, b_three, b_two = (b_ref[:, group, mat].reshape(width, width) for mat in range(3))
         for part in range(cap_rows // TERM_ROWS):
-            for copy in copies[group, part]:
-                copy.wait()
+            for arrival in arrivals(group, part, cap_rows // TERM_ROWS):
+                for copy in copies[group, arrival]:
+                    copy.wait()
             rows = slice(part * TERM_ROWS, (part + 1) * TERM_ROWS)
             k_part, err = k_ref[group, rows], e_ref[group, rows]
             h_one = dot(k_part, b_one, ((1,), (0,)))
             h_three = dot(k_part, b_three, ((1,), (0,)))
             back = dot(err, b_two, ((1,), (1,)))
-            sig = 0.5 * jnp.tanh(0.5 * h_one) + 0.5
-            gate = h_one * sig
+            half = 0.5 * h_one
+            turn = jnp.tanh(half)
+            gate = half * turn + half
+            sig = 0.5 * turn + 0.5
             a_ref[rows] = (gate * h_three).astype(jnp.bfloat16)
             d_ref[rows, :width] = (back * h_three * (sig + gate * (1.0 - sig))).astype(jnp.bfloat16)
             d_ref[rows, width:] = (back * gate).astype(jnp.bfloat16)
@@ -145,30 +156,30 @@
     )(k_flat, e_flat, halves)
 
 
-def apply_kernel(q_ref, c_ref, live_ref, scale_ref, o_ref, ssq_ref):
+def apply_kernel(q_ref, c_ref, scale_ref, o_ref, ssq_ref):
     groups = c_ref.shape[1]
     width = q_ref.shape[1] // groups
     tokens = q_ref.shape[0]
-    first = pl.program_id(0) * tokens
-    live = first + lax.broadcasted_iota(jnp.int32, (tokens, width), 0) < live_ref[0]
     squares = jnp.zeros((tokens, 128), jnp.float32)
     for group in range(groups):
         q_part = q_ref[:, group * width : (group + 1) * width]
         c_one, c_three, c_two = (c_ref[:, group, mat].reshape(width, width) for mat in range(3))
         q_one = dot(q_part, c_one, ((1,), (0,)))
         q_three = dot(q_part, c_three, ((1,), (0,)))
-        a_query = (q_one * (0.5 * jnp.tanh(0.5 * q_one) + 0.5) * q_three).astype(jnp.bfloat16)
-        o_part = dot(a_query, c_two, ((1,), (0,)))
-        o_part = jnp.where(live, o_part, 0.0).astype(jnp.bfloat16)
+        half = 0.5 * q_one
+        a_query = ((half * jnp.tanh(half) + half) * q_three).astype(jnp.bfloat16)
+        o_part = dot(a_query, c_two, ((1,), (0,))).astype(jnp.bfloat16)
         o_ref[:, group * width : (group + 1) * width] = o_part
-        scaled = o_part.astype(jnp.float32) * scale_ref[group]
-        scaled = scaled * scaled
-        for col in range(width // 128):
-            squares = squares + scaled[:, col * 128 : (col + 1) * 128]
+        wide = o_part.astype(jnp.float32)
+        wide = wide * wide
+        lanes = wide[:, :128]
+        for col in range(1, width // 128):
+            lanes = lanes + wide[:, col * 128 : (col + 1) * 128]
+        squares = squares + lanes * (scale_ref[group] * scale_ref[group])
     ssq_ref[...] = jnp.sum(squares.T, axis=0, keepdims=True)
 
 
-def apply(q_flat, fresh, own_count, scales):
+def apply(q_flat, fresh, scales):
     cap_rows, both = q_flat.shape
     steps = cap_rows // APPLY_ROWS
     tokens = pl.BlockSpec((APPLY_ROWS, both), lambda t: (t, 0))
@@ -179,7 +190,6 @@
             tokens,
             pl.BlockSpec(memory_space=pltpu.VMEM),
             pl.BlockSpec(memory_space=pltpu.SMEM),
-            pl.BlockSpec(memory_space=pltpu.SMEM),
         ],
         out_specs=[tokens, pl.BlockSpec((1, APPLY_ROWS), lambda t: (0, t))],
         out_shape=[
@@ -188,10 +198,10 @@
         ],
         compiler_params=params(APPLY_MIB),
         name="apply",
-    )(q_flat, fresh, own_count, scales)
-
-
-def finish_kernel(o_ref, ssq_ref, scale_ref, out):
+    )(q_flat, fresh, scales)
+
+
+def finish_kernel(o_ref, ssq_ref, scale_ref, live_ref, out):
     tokens, both = o_ref.shape
     groups = scale_ref.shape[0]
     width = both // groups
@@ -199,8 +209,10 @@
     tiles = width // lanes
     side = 256
     span = side // (groups * tiles)
-    total_sq = jnp.sum(ssq_ref[...], axis=0, keepdims=True)
+    total_sq = jnp.sum(ssq_ref[...], axis=0)
     factor = lax.rsqrt(total_sq * scale_ref[groups - 1, 1] + EPS)
+    place = pl.program_id(0) * tokens + lax.broadcasted_iota(jnp.int32, (1, tokens), 1)
+    factor = jnp.where(place < live_ref[0], factor, 0.0)
     factor = jnp.broadcast_to(factor, (lanes, tokens)).T
     columns = []
     for start in range(0, tokens, span):
@@ -221,7 +233,7 @@
         out[index * side : (index + 1) * side] = mixed[:, index * lanes : (index + 1) * lanes]
 
 
-def finish(fast, total_sq, scales):
+def finish(fast, total_sq, scales, own_count):
     cap_rows, both = fast.shape
     lanes = 128
     rows = FINISH_ROWS * both // lanes
@@ -230,14 +242,15 @@
         grid=(cap_rows // FINISH_ROWS,),
         in_specs=[
             pl.BlockSpec((FINISH_ROWS, both), lambda t: (t, 0)),
-            pl.BlockSpec((total_sq.shape[0], FINISH_ROWS), lambda t: (0, t)),
+            pl.BlockSpec((total_sq.shape[0], 1, FINISH_ROWS), lambda t: (0, 0, t)),
+            pl.BlockSpec(memory_space=pltpu.SMEM),
             pl.BlockSpec(memory_space=pltpu.SMEM),
         ],
         out_specs=pl.BlockSpec((rows, lanes), lambda t: (t, 0)),
         out_shape=jax.ShapeDtypeStruct((cap_rows * both // lanes, lanes), jnp.bfloat16),
         compiler_params=params(FINISH_MIB),
         name="finish",
-    )(fast, total_sq, scales)
+    )(fast, total_sq, scales, own_count)
 
 
 def exchange(blocks):
@@ -259,10 +272,10 @@
     flat = (cap_rows, groups * feat_width)
     sums = exchange(terms(key_rows.reshape(flat), err.reshape(flat), halves))
     fresh = exchange(renew(sums, weights))
-    fast, partial_sq = apply(queries.reshape(flat), fresh, own_count[None], group_scales)
-    total_sq = lax.all_gather(partial_sq, "heads", axis=0, tiled=True)
+    fast, partial_sq = apply(queries.reshape(flat), fresh, group_scales)
+    total_sq = lax.all_gather(partial_sq, "heads", axis=0)
     share = jnp.full_like(group_scales, 1.0 / (groups * feat_width * lax.axis_size("heads")))
-    ordered = finish(fast, total_sq, jnp.stack((group_scales, share), axis=1))
+    ordered = finish(fast, total_sq, jnp.stack((group_scales, share), axis=1), own_count[None])
     ordered = ordered.reshape(cap_rows, feat_width // 128, groups, 128).transpose(0, 2, 1, 3)
     return ordered.reshape(queries.shape)
 

time: 193 us -> 191 us (0.990)
    unnamed x18 -> x17, local copies, waits for them, and re-layouts: 12.4 us -> 11.8 us
where the time goes in v4:
time: 191 us; the launch traced here: 190 us
  waiting for transfers between devices  62.1 us (33%)
  blocking collectives  55.3 us (29%)
  Pallas kernels  38.4 us (20%)
  local copies, waits for them, and re-layouts  14.4 us (8%)
  starting transfers between devices  14.2 us (7%)
  other arithmetic  5.91 us (3%)
    all_to_all x2, waiting for transfers between devices, exchange(): return lax.all_to_all(blocks, 'seq', 0, 0, tiled=True)  62.1 us
    all_to_all x1, blocking collectives, exchange(): return lax.all_to_all(blocks, 'seq', 0, 0, tiled=True)  45.7 us
    pallas_call x1, Pallas kernels, terms(): pl.pallas_call(terms_kernel, in_specs=[pl.BlockSpec(memory_space=pl.ANY),...  17.1 us
    all_to_all x2, starting transfers between devices, exchange(): return lax.all_to_all(blocks, 'seq', 0, 0, tiled=True)  14.2 us
    unnamed x17, local copies, waits for them, and re-layouts  11.8 us
    pallas_call x1, Pallas kernels, apply(): pl.pallas_call(apply_kernel, grid=(steps,), in_specs=[tokens, pl.BlockSpe...  10.6 us
    all_gather x1, blocking collectives, shards(): total_sq = lax.all_gather(partial_sq, 'heads', axis=0)  9.67 us
    convert_element_type x1, other arithmetic, shards(): (eta[:, :, None] * value_rows.astype(jnp.float32)).astype(jnp.bfloat16)  5.35 us
  transfers between devices with their start and end apart: 2, of which 2 were waited for; matrix products, arithmetic and copies ran while one was open for 11% of the time, Pallas kernels for 0%

profile of v4, /device:TPU:1, one launch (start us, length us, event | category | flops | bytes accessed | tf_op | source)
XLA Modules:
  0.0 190.4 jit_solution(1629485640570759216)
XLA Ops:
  0.0 0.0 copy-start.6
  0.0 0.0 copy-start.5
  0.0 2.9 %spread.1 = bf16[32,2,3,16,512]{4,3,2,1,0:T(8,128)(2,1)} custom-call(f32[2,16,512]{2,1,0:T(8,128)} %w_first.3, f32[2,16,512]{2,1,0:T(8,128)} %w_third.3, f32[2,16,512]{2,1,0:T(8,128)} %w_second.3), custom_call_target="tpu_custom_call" | custom-call | tf_op jit(solution)/shard_map/spread/pallas_call | solution.py:43
  2.9 9.7 %all-to-all-start = ((bf16[32,2,3,16,512]{4,3,2,1,0:T(8,128)(2,1)}), bf16[32,2,3,16,512]{4,3,2,1,0:T(8,128)(2,1)S(1)}, u32[]{:S(2)}, u32[]{:S(2)}) async-start(bf16[32,2,3,16,512]{4,3,2,1,0:T(8,128)(2,1)} %spread.1), calls=%async_computation | async-start | bytes 6291456 | tf_op jit(solution)/shard_map/all_to_all | solution.py:257
  12.7 0.0 copy-done.6
  12.7 0.6 dynamic_slice.3.live_ref
  13.2 0.5 fusion
  13.8 0.0 copy-done.5
  13.8 1.3 copy.13
  15.2 5.4 %multiply_convert_fusion = bf16[2048,2,512]{2,1,0:T(2,128)(2,1)S(1)} fusion(bf16[2048,2,512]{2,1,0:T(2,128)(2,1)} %param.11, f32[2048,2]{1,0:T(8,128)} %copy.13), kind=kLoop, calls=%fused_computation | loop fusion | flops 6291456 | bytes 8404992 | tf_op jit(solution)/shard_map/convert_element_type | solution.py:271
  20.5 0.0 copy-start.4
  20.5 3.2 %copy.18 = bf16[256,8,2,512]{3,1,2,0:T(8,128)(2,1)} copy(bf16[256,8,2,512]{3,2,1,0:T(2,128)(2,1)S(1)} %bitcast.21) | data formatting | bytes 8388608
  23.7 0.0 copy-done.4
  23.7 3.2 %copy.17 = bf16[256,8,2,512]{3,1,2,0:T(8,128)(2,1)} copy(bf16[256,8,2,512]{3,2,1,0:T(2,128)(2,1)S(1)} %bitcast.22) | data formatting | bytes 8388608
  26.9 26.8 %all-to-all-done.b_ref = bf16[32,2,3,16,512]{4,3,2,1,0:T(8,128)(2,1)S(1)} async-done(((bf16[32,2,3,16,512]{4,3,2,1,0:T(8,128)(2,1)}), bf16[32,2,3,16,512]{4,3,2,1,0:T(8,128)(2,1)S(1)}, u32[]{:S(2)}, u32[]{:S(2)}) %all-to-all-start) | async-done | bytes 3145760 | tf_op jit(solution)/shard_map/all_to_all | solution.py:257
  53.7 17.1 %terms.1 = bf16[32,2,3,16,512]{4,3,2,1,0:T(8,128)(2,1)S(1)} custom-call(bf16[2048,1024]{1,0:T(8,128)(2,1)} %bitcast.19, bf16[2048,1024]{1,0:T(8,128)(2,1)} %bitcast.18, bf16[32,2,3,16,512]{4,3,2,1,0:T(8,128)(2,1)S(1)} %all-to-all-done.b_ref), custom_call_target="tpu_custom_call" | custom-call | tf_op jit(solution)/shard_map/terms/pallas_call | solution.py:137
  70.8 0.0 copy-start
  70.8 0.0 copy-start.1
  70.8 0.0 copy-start.2
  70.8 45.7 %all_to_all.15.blocks = bf16[32,2,3,16,512]{4,3,2,1,0:T(8,128)(2,1)S(1)} all-to-all(bf16[32,2,3,16,512]{4,3,2,1,0:T(8,128)(2,1)S(1)} %terms.1), channel_id=1, replica_groups=mesh['heads'=4,'seq'=32] {'seq'}, dimensions={0} | all-to-all | bytes 6291456 | tf_op jit(solution)/shard_map/all_to_all | solution.py:257
  116.5 0.0 copy-done
  116.5 0.0 copy-done.1
  116.5 0.0 copy-done.2
  116.5 2.5 %renew.1 = bf16[32,2,3,16,512]{4,3,2,1,0:T(8,128)(2,1)} custom-call(bf16[32,2,3,16,512]{4,3,2,1,0:T(8,128)(2,1)S(1)} %all_to_all.15.blocks, f32[2,16,512]{2,1,0:T(8,128)S(1)} %copy-done, f32[2,16,512]{2,1,0:T(8,128)S(1)} %copy-done.1, f32[2,16,512]{2,1,0:T(8,128)S(1)} %copy-done.2), custom_call_target="tpu_custom_call" | custom-call | tf_op jit(solution)/shard_map/renew/pallas_call | solution.py:71
  119.0 4.5 %all-to-all-start.2 = ((bf16[32,2,3,16,512]{4,3,2,1,0:T(8,128)(2,1)}), bf16[32,2,3,16,512]{4,3,2,1,0:T(8,128)(2,1)S(1)}, u32[]{:S(2)}, u32[]{:S(2)}) async-start(bf16[32,2,3,16,512]{4,3,2,1,0:T(8,128)(2,1)} %renew.1), calls=%async_computation.2 | async-start | bytes 6291456 | tf_op jit(solution)/shard_map/all_to_all | solution.py:257
  123.5 0.0 copy-start.3
  123.5 5.4 %copy.16 = bf16[256,8,2,512]{3,1,2,0:T(8,128)(2,1)} copy(bf16[256,8,2,512]{3,2,1,0:T(2,128)(2,1)} %bitcast.23) | data formatting | bytes 8388608
  128.9 0.0 copy-done.3
  128.9 0.1 copy.14
  129.0 0.6 stack.7.scale_ref
  129.5 35.2 %all-to-all-done.2.c_ref = bf16[32,2,3,16,512]{4,3,2,1,0:T(8,128)(2,1)S(1)} async-done(((bf16[32,2,3,16,512]{4,3,2,1,0:T(8,128)(2,1)}), bf16[32,2,3,16,512]{4,3,2,1,0:T(8,128)(2,1)S(1)}, u32[]{:S(2)}, u32[]{:S(2)}) %all-to-all-start.2) | async-done | bytes 3145760 | tf_op jit(solution)/shard_map/all_to_all | solution.py:257
  164.8 10.6 %apply.1 = (bf16[2048,1024]{1,0:T(8,128)(2,1)}, f32[1,2048]{1,0:T(1,128)S(1)}) custom-call(bf16[2048,1024]{1,0:T(8,128)(2,1)} %bitcast.20, bf16[32,2,3,16,512]{4,3,2,1,0:T(8,128)(2,1)S(1)} %all-to-all-done.2.c_ref, f32[2]{0:T(128)S(1)} %copy-done.3), custom_call_target="tpu_custom_call" | custom-call | tf_op jit(solution)/shard_map/apply/pallas_call | solution.py:186
  175.4 9.7 %all-gather.1.ssq_ref = f32[4,1,2048]{2,1,0:T(1,128)} all-gather(f32[1,1,2048]{2,1,0:T(1,128)S(1)} %bitcast.16), channel_id=2, replica_groups=mesh['heads'=4,'seq'=32] {'heads'}, dimensions={0}, use_global_device_ids=true | all-gather | bytes 40960 | tf_op jit(solution)/shard_map/all_gather | solution.py:276
  185.1 5.3 %finish.1 = bf16[16384,128]{1,0:T(8,128)(2,1)} custom-call(bf16[2048,1024]{1,0:T(8,128)(2,1)} %get-tuple-element.7.o_ref, f32[4,1,2048]{2,1,0:T(1,128)} %all-gather.1.ssq_ref, f32[2,2]{1,0:T(2,128)} %stack.7.scale_ref, s32[1]{0:T(128)} %dynamic_slice.3.live_ref), custom_call_target="tpu_custom_call" | custom-call | tf_op jit(solution)/shard_map/finish/pallas_call | solution.py:240
  (1 shorter events, 0.0 us)
Async XLA Ops:
  0.0 12.7 %copy-start.6 = (s32[32]{0:T(128)S(1)}, s32[32]{0:T(128)}, u32[]{:S(2)}) copy-start(s32[32]{0:T(128)} %param.13) | copy-start | bytes 388
  0.0 13.8 %copy-start.5 = (bf16[2,2048]{1,0:T(2,128)(2,1)S(1)}, bf16[2,2048]{1,0:T(2,128)(2,1)}, u32[]{:S(2)}) copy-start(bf16[2,2048]{1,0:T(2,128)(2,1)} %param.12) | copy-start | bytes 24580
  2.9 50.8 %all-to-all-start = ((bf16[32,2,3,16,512]{4,3,2,1,0:T(8,128)(2,1)}), bf16[32,2,3,16,512]{4,3,2,1,0:T(8,128)(2,1)S(1)}, u32[]{:S(2)}, u32[]{:S(2)}) async-start(bf16[32,2,3,16,512]{4,3,2,1,0:T(8,128)(2,1)} %spread.1), calls=%async_computation | async-start | bytes 6291456 | tf_op jit(solution)/shard_map/all_to_all | solution.py:257
  20.5 3.2 %copy-start.4 = (bf16[2048,2,512]{2,1,0:T(2,128)(2,1)S(1)}, bf16[2048,2,512]{2,1,0:T(2,128)(2,1)}, u32[]{:S(2)}) copy-start(bf16[2048,2,512]{2,1,0:T(2,128)(2,1)} %param.10) | copy-start | bytes 12582916
  70.8 45.7 %copy-start = (f32[2,16,512]{2,1,0:T(8,128)S(1)}, f32[2,16,512]{2,1,0:T(8,128)}, u32[]{:S(2)}) copy-start(f32[2,16,512]{2,1,0:T(8,128)} %w_first.3) | copy-start | bytes 196612
  70.8 45.7 %copy-start.1 = (f32[2,16,512]{2,1,0:T(8,128)S(1)}, f32[2,16,512]{2,1,0:T(8,128)}, u32[]{:S(2)}) copy-start(f32[2,16,512]{2,1,0:T(8,128)} %w_third.3) | copy-start | bytes 196612
  70.8 45.7 %copy-start.2 = (f32[2,16,512]{2,1,0:T(8,128)S(1)}, f32[2,16,512]{2,1,0:T(8,128)}, u32[]{:S(2)}) copy-start(f32[2,16,512]{2,1,0:T(8,128)} %w_second.3) | copy-start | bytes 196612
  119.0 45.8 %all-to-all-start.2 = ((bf16[32,2,3,16,512]{4,3,2,1,0:T(8,128)(2,1)}), bf16[32,2,3,16,512]{4,3,2,1,0:T(8,128)(2,1)S(1)}, u32[]{:S(2)}, u32[]{:S(2)}) async-start(bf16[32,2,3,16,512]{4,3,2,1,0:T(8,128)(2,1)} %renew.1), calls=%async_computation.2 | async-start | bytes 6291456 | tf_op jit(solution)/shard_map/all_to_all | solution.py:257
  123.5 5.4 %copy-start.3 = (f32[2]{0:T(128)S(1)}, f32[2]{0:T(128)}, u32[]{:S(2)}) copy-start(f32[2]{0:T(128)} %scale_ref.1) | copy-start | bytes 28

commit v5 on v4

--- a/solution.py
+++ b/solution.py
@@ -10,8 +10,8 @@
 TERM_ROWS = 512
 SPREAD_MIB = 60
 TERMS_MIB = 46
-APPLY_MIB = 50
-FINISH_MIB = 58
+APPLY_MIB = 44
+FINISH_MIB = 40
 APPLY_ROWS = 512
 FINISH_ROWS = 1024
 
@@ -160,6 +160,7 @@
     groups = c_ref.shape[1]
     width = q_ref.shape[1] // groups
     tokens = q_ref.shape[0]
+    own_rows = pl.ds(pl.multiple_of(pl.program_id(0) * tokens, tokens), tokens)
     squares = jnp.zeros((tokens, 128), jnp.float32)
     for group in range(groups):
         q_part = q_ref[:, group * width : (group + 1) * width]
@@ -169,7 +170,7 @@
         half = 0.5 * q_one
         a_query = ((half * jnp.tanh(half) + half) * q_three).astype(jnp.bfloat16)
         o_part = dot(a_query, c_two, ((1,), (0,))).astype(jnp.bfloat16)
-        o_ref[:, group * width : (group + 1) * width] = o_part
+        o_ref[own_rows, group * width : (group + 1) * width] = o_part
         wide = o_part.astype(jnp.float32)
         wide = wide * wide
         lanes = wide[:, :128]
@@ -191,7 +192,10 @@
             pl.BlockSpec(memory_space=pltpu.VMEM),
             pl.BlockSpec(memory_space=pltpu.SMEM),
         ],
-        out_specs=[tokens, pl.BlockSpec((1, APPLY_ROWS), lambda t: (0, t))],
+        out_specs=[
+            pl.BlockSpec(memory_space=pltpu.VMEM),
+            pl.BlockSpec((1, APPLY_ROWS), lambda t: (0, t)),
+        ],
         out_shape=[
             jax.ShapeDtypeStruct(q_flat.shape, jnp.bfloat16),
             jax.ShapeDtypeStruct((1, cap_rows), jnp.float32),
@@ -202,7 +206,8 @@
 
 
 def finish_kernel(o_ref, ssq_ref, scale_ref, live_ref, out):
-    tokens, both = o_ref.shape
+    tokens, both = FINISH_ROWS, o_ref.shape[1]
+    base = pl.multiple_of(pl.program_id(0) * tokens, tokens)
     groups = scale_ref.shape[0]
     width = both // groups
     lanes = 128
@@ -221,7 +226,7 @@
         for group in range(groups):
             for tile in range(tiles):
                 col = group * width + tile * lanes
-                part = o_ref[rows, col : col + lanes].astype(jnp.float32) * scale_ref[group, 0]
+                part = o_ref[pl.ds(base + start, span), col : col + lanes].astype(jnp.float32) * scale_ref[group, 0]
                 pieces.append(part * factor[rows])
         columns.append(jnp.concatenate(pieces, axis=0).astype(jnp.bfloat16))
     row = lax.broadcasted_iota(jnp.int32, (side, side), 0)
@@ -241,7 +246,7 @@
         finish_kernel,
         grid=(cap_rows // FINISH_ROWS,),
         in_specs=[
-            pl.BlockSpec((FINISH_ROWS, both), lambda t: (t, 0)),
+            pl.BlockSpec(memory_space=pltpu.VMEM),
             pl.BlockSpec((total_sq.shape[0], 1, FINISH_ROWS), lambda t: (0, 0, t)),
             pl.BlockSpec(memory_space=pltpu.SMEM),
             pl.BlockSpec(memory_space=pltpu.SMEM),

time: 191 us -> 189 us (0.990)
  transfers between devices with their start and end apart: 2 -> 2, of which waited for: 2 -> 2; matrix products, arithmetic and copies ran while one was open for 11% -> 10% of each run, Pallas kernels for 0% -> 0%
where the time goes in v5:
time: 189 us; the launch traced here: 188 us
  waiting for transfers between devices  62.6 us (33%)
  blocking collectives  54.9 us (29%)
  Pallas kernels  36.5 us (19%)
  starting transfers between devices  14.2 us (8%)
  local copies, waits for them, and re-layouts  13.8 us (7%)
  other arithmetic  5.91 us (3%)
    all_to_all x2, waiting for transfers between devices, exchange(): return lax.all_to_all(blocks, 'seq', 0, 0, tiled=True)  62.6 us
    all_to_all x1, blocking collectives, exchange(): return lax.all_to_all(blocks, 'seq', 0, 0, tiled=True)  45.7 us
    pallas_call x1, Pallas kernels, terms(): pl.pallas_call(terms_kernel, in_specs=[pl.BlockSpec(memory_space=pl.ANY),...  17.1 us
    all_to_all x2, starting transfers between devices, exchange(): return lax.all_to_all(blocks, 'seq', 0, 0, tiled=True)  14.2 us
    unnamed x17, local copies, waits for them, and re-layouts  11.8 us
    pallas_call x1, Pallas kernels, apply(): pl.pallas_call(apply_kernel, grid=(steps,), in_specs=[tokens, pl.BlockSpe...  9.81 us
    all_gather x1, blocking collectives, shards(): total_sq = lax.all_gather(partial_sq, 'heads', axis=0)  9.24 us
    convert_element_type x1, other arithmetic, shards(): (eta[:, :, None] * value_rows.astype(jnp.float32)).astype(jnp.bfloat16)  5.35 us
  transfers between devices with their start and end apart: 2, of which 2 were waited for; matrix products, arithmetic and copies ran while one was open for 10% of the time, Pallas kernels for 0%

profile of v5, /device:TPU:1, one launch (start us, length us, event | category | flops | bytes accessed | tf_op | source)
XLA Modules:
  0.0 188.1 jit_solution(15356435803874314363)
XLA Ops:
  0.0 0.0 copy-start.6
  0.0 0.0 copy-start.5
  0.0 2.9 %spread.1 = bf16[32,2,3,16,512]{4,3,2,1,0:T(8,128)(2,1)} custom-call(f32[2,16,512]{2,1,0:T(8,128)} %w_first.3, f32[2,16,512]{2,1,0:T(8,128)} %w_third.3, f32[2,16,512]{2,1,0:T(8,128)} %w_second.3), custom_call_target="tpu_custom_call" | custom-call | tf_op jit(solution)/shard_map/spread/pallas_call | solution.py:43
  2.9 9.7 %all-to-all-start = ((bf16[32,2,3,16,512]{4,3,2,1,0:T(8,128)(2,1)}), bf16[32,2,3,16,512]{4,3,2,1,0:T(8,128)(2,1)S(1)}, u32[]{:S(2)}, u32[]{:S(2)}) async-start(bf16[32,2,3,16,512]{4,3,2,1,0:T(8,128)(2,1)} %spread.1), calls=%async_computation | async-start | bytes 6291456 | tf_op jit(solution)/shard_map/all_to_all | solution.py:262
  12.7 0.0 copy-done.6
  12.7 0.6 dynamic_slice.3.live_ref
  13.2 0.5 fusion
  13.8 0.0 copy-done.5
  13.8 1.3 copy.13
  15.2 5.4 %multiply_convert_fusion = bf16[2048,2,512]{2,1,0:T(2,128)(2,1)S(1)} fusion(bf16[2048,2,512]{2,1,0:T(2,128)(2,1)} %param.11, f32[2048,2]{1,0:T(8,128)} %copy.13), kind=kLoop, calls=%fused_computation | loop fusion | flops 6291456 | bytes 8404992 | tf_op jit(solution)/shard_map/convert_element_type | solution.py:276
  20.5 0.0 copy-start.4
  20.5 3.2 %copy.18 = bf16[256,8,2,512]{3,1,2,0:T(8,128)(2,1)} copy(bf16[256,8,2,512]{3,2,1,0:T(2,128)(2,1)S(1)} %bitcast.21) | data formatting | bytes 8388608
  23.7 0.0 copy-done.4
  23.7 3.2 %copy.17 = bf16[256,8,2,512]{3,1,2,0:T(8,128)(2,1)} copy(bf16[256,8,2,512]{3,2,1,0:T(2,128)(2,1)S(1)} %bitcast.22) | data formatting | bytes 8388608
  26.9 26.8 %all-to-all-done.b_ref = bf16[32,2,3,16,512]{4,3,2,1,0:T(8,128)(2,1)S(1)} async-done(((bf16[32,2,3,16,512]{4,3,2,1,0:T(8,128)(2,1)}), bf16[32,2,3,16,512]{4,3,2,1,0:T(8,128)(2,1)S(1)}, u32[]{:S(2)}, u32[]{:S(2)}) %all-to-all-start) | async-done | bytes 3145760 | tf_op jit(solution)/shard_map/all_to_all | solution.py:262
  53.7 17.1 %terms.1 = bf16[32,2,3,16,512]{4,3,2,1,0:T(8,128)(2,1)S(1)} custom-call(bf16[2048,1024]{1,0:T(8,128)(2,1)} %bitcast.19, bf16[2048,1024]{1,0:T(8,128)(2,1)} %bitcast.18, bf16[32,2,3,16,512]{4,3,2,1,0:T(8,128)(2,1)S(1)} %all-to-all-done.b_ref), custom_call_target="tpu_custom_call" | custom-call | tf_op jit(solution)/shard_map/terms/pallas_call | solution.py:137
  70.8 0.0 copy-start
  70.8 0.0 copy-start.1
  70.8 0.0 copy-start.2
  70.8 45.7 %all_to_all.15.blocks = bf16[32,2,3,16,512]{4,3,2,1,0:T(8,128)(2,1)S(1)} all-to-all(bf16[32,2,3,16,512]{4,3,2,1,0:T(8,128)(2,1)S(1)} %terms.1), channel_id=1, replica_groups=mesh['heads'=4,'seq'=32] {'seq'}, dimensions={0} | all-to-all | bytes 6291456 | tf_op jit(solution)/shard_map/all_to_all | solution.py:262
  116.5 0.0 copy-done
  116.5 0.0 copy-done.1
  116.5 0.0 copy-done.2
  116.5 2.5 %renew.1 = bf16[32,2,3,16,512]{4,3,2,1,0:T(8,128)(2,1)} custom-call(bf16[32,2,3,16,512]{4,3,2,1,0:T(8,128)(2,1)S(1)} %all_to_all.15.blocks, f32[2,16,512]{2,1,0:T(8,128)S(1)} %copy-done, f32[2,16,512]{2,1,0:T(8,128)S(1)} %copy-done.1, f32[2,16,512]{2,1,0:T(8,128)S(1)} %copy-done.2), custom_call_target="tpu_custom_call" | custom-call | tf_op jit(solution)/shard_map/renew/pallas_call | solution.py:71
  119.0 4.5 %all-to-all-start.2 = ((bf16[32,2,3,16,512]{4,3,2,1,0:T(8,128)(2,1)}), bf16[32,2,3,16,512]{4,3,2,1,0:T(8,128)(2,1)S(1)}, u32[]{:S(2)}, u32[]{:S(2)}) async-start(bf16[32,2,3,16,512]{4,3,2,1,0:T(8,128)(2,1)} %renew.1), calls=%async_computation.2 | async-start | bytes 6291456 | tf_op jit(solution)/shard_map/all_to_all | solution.py:262
  123.5 0.0 copy-start.3
  123.5 5.4 %copy.16 = bf16[256,8,2,512]{3,1,2,0:T(8,128)(2,1)} copy(bf16[256,8,2,512]{3,2,1,0:T(2,128)(2,1)} %bitcast.23) | data formatting | bytes 8388608
  128.9 0.0 copy-done.3
  128.9 0.1 copy.14
  129.0 35.8 %all-to-all-done.2.c_ref = bf16[32,2,3,16,512]{4,3,2,1,0:T(8,128)(2,1)S(1)} async-done(((bf16[32,2,3,16,512]{4,3,2,1,0:T(8,128)(2,1)}), bf16[32,2,3,16,512]{4,3,2,1,0:T(8,128)(2,1)S(1)}, u32[]{:S(2)}, u32[]{:S(2)}) %all-to-all-start.2) | async-done | bytes 3145760 | tf_op jit(solution)/shard_map/all_to_all | solution.py:262
  164.8 9.8 %apply.1 = (bf16[2048,1024]{1,0:T(8,128)(2,1)S(1)}, f32[1,2048]{1,0:T(1,128)S(1)}) custom-call(bf16[2048,1024]{1,0:T(8,128)(2,1)} %bitcast.20, bf16[32,2,3,16,512]{4,3,2,1,0:T(8,128)(2,1)S(1)} %all-to-all-done.2.c_ref, f32[2]{0:T(128)S(1)} %copy-done.3), custom_call_target="tpu_custom_call" | custom-call | tf_op jit(solution)/shard_map/apply/pallas_call | solution.py:187
  174.6 9.2 %all-gather.1.ssq_ref = f32[4,1,2048]{2,1,0:T(1,128)S(1)} all-gather(f32[1,1,2048]{2,1,0:T(1,128)S(1)} %bitcast.16), channel_id=2, replica_groups=mesh['heads'=4,'seq'=32] {'heads'}, dimensions={0}, use_global_device_ids=true | all-gather | bytes 40960 | tf_op jit(solution)/shard_map/all_gather | solution.py:281
  183.8 4.3 %finish.1 = bf16[16384,128]{1,0:T(8,128)(2,1)} custom-call(bf16[2048,1024]{1,0:T(8,128)(2,1)S(1)} %get-tuple-element.7.o_ref, f32[4,1,2048]{2,1,0:T(1,128)S(1)} %all-gather.1.ssq_ref, f32[2,2]{1,0:T(2,128)S(1)} %stack.7.scale_ref, s32[1]{0:T(128)} %dynamic_slice.3.live_ref), custom_call_target="tpu_custom_call" | custom-call | tf_op jit(solution)/shard_map/finish/pallas_call | solution.py:245
  (2 shorter events, 0.0 us)
Async XLA Ops:
  0.0 12.7 %copy-start.6 = (s32[32]{0:T(128)S(1)}, s32[32]{0:T(128)}, u32[]{:S(2)}) copy-start(s32[32]{0:T(128)} %param.13) | copy-start | bytes 388
  0.0 13.8 %copy-start.5 = (bf16[2,2048]{1,0:T(2,128)(2,1)S(1)}, bf16[2,2048]{1,0:T(2,128)(2,1)}, u32[]{:S(2)}) copy-start(bf16[2,2048]{1,0:T(2,128)(2,1)} %param.12) | copy-start | bytes 24580
  2.9 50.8 %all-to-all-start = ((bf16[32,2,3,16,512]{4,3,2,1,0:T(8,128)(2,1)}), bf16[32,2,3,16,512]{4,3,2,1,0:T(8,128)(2,1)S(1)}, u32[]{:S(2)}, u32[]{:S(2)}) async-start(bf16[32,2,3,16,512]{4,3,2,1,0:T(8,128)(2,1)} %spread.1), calls=%async_computation | async-start | bytes 6291456 | tf_op jit(solution)/shard_map/all_to_all | solution.py:262
  20.5 3.2 %copy-start.4 = (bf16[2048,2,512]{2,1,0:T(2,128)(2,1)S(1)}, bf16[2048,2,512]{2,1,0:T(2,128)(2,1)}, u32[]{:S(2)}) copy-start(bf16[2048,2,512]{2,1,0:T(2,128)(2,1)} %param.10) | copy-start | bytes 12582916
  70.8 45.7 %copy-start = (f32[2,16,512]{2,1,0:T(8,128)S(1)}, f32[2,16,512]{2,1,0:T(8,128)}, u32[]{:S(2)}) copy-start(f32[2,16,512]{2,1,0:T(8,128)} %w_first.3) | copy-start | bytes 196612
  70.8 45.7 %copy-start.1 = (f32[2,16,512]{2,1,0:T(8,128)S(1)}, f32[2,16,512]{2,1,0:T(8,128)}, u32[]{:S(2)}) copy-start(f32[2,16,512]{2,1,0:T(8,128)} %w_third.3) | copy-start | bytes 196612
  70.8 45.7 %copy-start.2 = (f32[2,16,512]{2,1,0:T(8,128)S(1)}, f32[2,16,512]{2,1,0:T(8,128)}, u32[]{:S(2)}) copy-start(f32[2,16,512]{2,1,0:T(8,128)} %w_second.3) | copy-start | bytes 196612
  119.0 45.8 %all-to-all-start.2 = ((bf16[32,2,3,16,512]{4,3,2,1,0:T(8,128)(2,1)}), bf16[32,2,3,16,512]{4,3,2,1,0:T(8,128)(2,1)S(1)}, u32[]{:S(2)}, u32[]{:S(2)}) async-start(bf16[32,2,3,16,512]{4,3,2,1,0:T(8,128)(2,1)} %renew.1), calls=%async_computation.2 | async-start | bytes 6291456 | tf_op jit(solution)/shard_map/all_to_all | solution.py:262
  123.5 5.4 %copy-start.3 = (f32[2]{0:T(128)S(1)}, f32[2]{0:T(128)}, u32[]{:S(2)}) copy-start(f32[2]{0:T(128)} %scale_ref.1) | copy-start | bytes 28

commit v6 on v5

--- a/solution.py
+++ b/solution.py
@@ -205,7 +205,7 @@
     )(q_flat, fresh, scales)
 
 
-def finish_kernel(o_ref, ssq_ref, scale_ref, live_ref, out):
+def finish_kernel(share, o_ref, ssq_ref, scale_ref, live_ref, out):
     tokens, both = FINISH_ROWS, o_ref.shape[1]
     base = pl.multiple_of(pl.program_id(0) * tokens, tokens)
     groups = scale_ref.shape[0]
@@ -215,7 +215,7 @@
     side = 256
     span = side // (groups * tiles)
     total_sq = jnp.sum(ssq_ref[...], axis=0)
-    factor = lax.rsqrt(total_sq * scale_ref[groups - 1, 1] + EPS)
+    factor = lax.rsqrt(total_sq * share + EPS)
     place = pl.program_id(0) * tokens + lax.broadcasted_iota(jnp.int32, (1, tokens), 1)
     factor = jnp.where(place < live_ref[0], factor, 0.0)
     factor = jnp.broadcast_to(factor, (lanes, tokens)).T
@@ -226,7 +226,7 @@
         for group in range(groups):
             for tile in range(tiles):
                 col = group * width + tile * lanes
-                part = o_ref[pl.ds(base + start, span), col : col + lanes].astype(jnp.float32) * scale_ref[group, 0]
+                part = o_ref[pl.ds(base + start, span), col : col + lanes].astype(jnp.float32) * scale_ref[group]
                 pieces.append(part * factor[rows])
         columns.append(jnp.concatenate(pieces, axis=0).astype(jnp.bfloat16))
     row = lax.broadcasted_iota(jnp.int32, (side, side), 0)
@@ -238,12 +238,12 @@
         out[index * side : (index + 1) * side] = mixed[:, index * lanes : (index + 1) * lanes]
 
 
-def finish(fast, total_sq, scales, own_count):
+def finish(fast, total_sq, scales, own_count, share):
     cap_rows, both = fast.shape
     lanes = 128
     rows = FINISH_ROWS * both // lanes
     return pl.pallas_call(
-        finish_kernel,
+        functools.partial(finish_kernel, share),
         grid=(cap_rows // FINISH_ROWS,),
         in_specs=[
             pl.BlockSpec(memory_space=pltpu.VMEM),
@@ -275,12 +275,13 @@
     eta = step_rates.T.astype(jnp.float32) * live_mask.astype(jnp.float32)[:, None] / root_total
     err = (eta[:, :, None] * value_rows.astype(jnp.float32)).astype(jnp.bfloat16)
     flat = (cap_rows, groups * feat_width)
+    q_flat, halves = lax.optimization_barrier((queries.reshape(flat), halves))
     sums = exchange(terms(key_rows.reshape(flat), err.reshape(flat), halves))
     fresh = exchange(renew(sums, weights))
-    fast, partial_sq = apply(queries.reshape(flat), fresh, group_scales)
+    fast, partial_sq = apply(q_flat, fresh, group_scales)
     total_sq = lax.all_gather(partial_sq, "heads", axis=0)
-    share = jnp.full_like(group_scales, 1.0 / (groups * feat_width * lax.axis_size("heads")))
-    ordered = finish(fast, total_sq, jnp.stack((group_scales, share), axis=1), own_count[None])
+    share = 1.0 / (groups * feat_width * lax.axis_size("heads"))
+    ordered = finish(fast, total_sq, group_scales, own_count[None], share)
     ordered = ordered.reshape(cap_rows, feat_width // 128, groups, 128).transpose(0, 2, 1, 3)
     return ordered.reshape(queries.shape)
 

time: 189 us -> 188 us (level)
  blocking collectives: 54.9 us -> 97.6 us
  waiting for transfers between devices: 62.6 us -> 23.5 us
  starting transfers between devices: 14.2 us -> 9.74 us
  Pallas kernels: 36.5 us -> 39.4 us
  local copies, waits for them, and re-layouts: 13.8 us -> 11.6 us
    all_to_all x1 -> x2, blocking collectives: 45.7 us -> 89 us  [exchange(): return lax.all_to_all(blocks, 'seq', 0, 0, tiled=True)]
    all_to_all x2 -> x1, waiting for transfers between devices: 62.6 us -> 23.5 us  [exchange(): return lax.all_to_all(blocks, 'seq', 0, 0, tiled=True)]
    all_to_all x2 -> x1, starting transfers between devices: 14.2 us -> 9.74 us  [exchange(): return lax.all_to_all(blocks, 'seq', 0, 0, tiled=True)]
    pallas_call x1, Pallas kernels: 2.48 us -> 4.95 us  [renew(): pl.pallas_call(renew_kernel, out_specs=pl.BlockSpec(memory_space=pl.ANY),...]
    unnamed x17 -> x19, local copies, waits for them, and re-layouts: 11.8 us -> 9.58 us
  transfers between devices with their start and end apart: 2 -> 1, of which waited for: 2 -> 1; matrix products, arithmetic and copies ran while one was open for 10% -> 9% of each run, Pallas kernels for 0% -> 0%
where the time goes in v6:
time: 188 us
  blocking collectives  97.6 us (52%)
  Pallas kernels  39.4 us (21%)
  waiting for transfers between devices  23.5 us (12%)
  local copies, waits for them, and re-layouts  11.6 us (6%)
  starting transfers between devices  9.74 us (5%)
  other arithmetic  5.99 us (3%)
    all_to_all x2, blocking collectives, exchange(): return lax.all_to_all(blocks, 'seq', 0, 0, tiled=True)  89 us
    all_to_all x1, waiting for transfers between devices, exchange(): return lax.all_to_all(blocks, 'seq', 0, 0, tiled=True)  23.5 us
    pallas_call x1, Pallas kernels, terms(): pl.pallas_call(terms_kernel, in_specs=[pl.BlockSpec(memory_space=pl.ANY),...  17.1 us
    pallas_call x1, Pallas kernels, apply(): pl.pallas_call(apply_kernel, grid=(steps,), in_specs=[tokens, pl.BlockSpe...  10 us
    all_to_all x1, starting transfers between devices, exchange(): return lax.all_to_all(blocks, 'seq', 0, 0, tiled=True)  9.74 us
    unnamed x19, local copies, waits for them, and re-layouts  9.58 us
    all_gather x1, blocking collectives, shards(): total_sq = lax.all_gather(partial_sq, 'heads', axis=0)  8.69 us
    convert_element_type x1, other arithmetic, shards(): (eta[:, :, None] * value_rows.astype(jnp.float32)).astype(jnp.bfloat16)  5.35 us
  transfers between devices with their start and end apart: 1, of which 1 were waited for; matrix products, arithmetic and copies ran while one was open for 9% of the time, Pallas kernels for 0%

profile of v6, /device:TPU:1, one launch (start us, length us, event | category | flops | bytes accessed | tf_op | source)
XLA Modules:
  0.0 187.9 jit_solution(2254734927064966417)
XLA Ops:
  0.0 0.0 copy-start.7
  0.0 0.0 copy-start.6
  0.0 2.9 %spread.1 = bf16[32,2,3,16,512]{4,3,2,1,0:T(8,128)(2,1)} custom-call(f32[2,16,512]{2,1,0:T(8,128)} %w_first.3, f32[2,16,512]{2,1,0:T(8,128)} %w_third.3, f32[2,16,512]{2,1,0:T(8,128)} %w_second.3), custom_call_target="tpu_custom_call" | custom-call | tf_op jit(solution)/shard_map/spread/pallas_call | solution.py:43
  3.0 9.7 %all-to-all-start = ((bf16[32,2,3,16,512]{4,3,2,1,0:T(8,128)(2,1)}), bf16[32,2,3,16,512]{4,3,2,1,0:T(8,128)(2,1)S(1)}, u32[]{:S(2)}, u32[]{:S(2)}) async-start(bf16[32,2,3,16,512]{4,3,2,1,0:T(8,128)(2,1)} %spread.1), calls=%async_computation | async-start | bytes 6291456 | tf_op jit(solution)/shard_map/all_to_all | solution.py:262
  12.7 0.0 copy-done.7
  12.7 0.6 dynamic_slice.3.live_ref
  13.4 0.6 fusion
  14.0 0.0 copy-done.6
  14.0 1.3 copy.12
  15.4 5.4 %multiply_convert_fusion = bf16[2048,2,512]{2,1,0:T(2,128)(2,1)S(1)} fusion(bf16[2048,2,512]{2,1,0:T(2,128)(2,1)} %param.11, f32[2048,2]{1,0:T(8,128)} %copy.12), kind=kLoop, calls=%fused_computation | loop fusion | flops 6291456 | bytes 8404992 | tf_op jit(solution)/shard_map/convert_element_type | solution.py:276
  20.7 0.0 copy-start.4
  20.7 3.2 %copy.16 = bf16[256,8,2,512]{3,1,2,0:T(8,128)(2,1)} copy(bf16[256,8,2,512]{3,2,1,0:T(2,128)(2,1)S(1)} %bitcast.19) | data formatting | bytes 8388608
  23.9 0.0 copy-done.4
  23.9 0.0 copy-start.5
  23.9 3.2 %copy.14 = bf16[256,8,2,512]{3,1,2,0:T(8,128)(2,1)} copy(bf16[256,8,2,512]{3,2,1,0:T(2,128)(2,1)S(1)} %bitcast.20) | data formatting | bytes 8388608
  27.1 0.0 copy-done.5
  27.1 3.1 %copy.15 = bf16[256,8,2,512]{3,1,2,0:T(8,128)(2,1)} copy(bf16[256,8,2,512]{3,2,1,0:T(2,128)(2,1)S(1)} %bitcast.21) | data formatting | bytes 8388608
  30.3 23.5 %all-to-all-done.b_ref = bf16[32,2,3,16,512]{4,3,2,1,0:T(8,128)(2,1)S(1)} async-done(((bf16[32,2,3,16,512]{4,3,2,1,0:T(8,128)(2,1)}), bf16[32,2,3,16,512]{4,3,2,1,0:T(8,128)(2,1)S(1)}, u32[]{:S(2)}, u32[]{:S(2)}) %all-to-all-start) | async-done | bytes 3145760 | tf_op jit(solution)/shard_map/all_to_all | solution.py:262
  53.8 17.1 %terms.1 = bf16[32,2,3,16,512]{4,3,2,1,0:T(8,128)(2,1)S(1)} custom-call(bf16[2048,1024]{1,0:T(8,128)(2,1)} %bitcast.17, bf16[2048,1024]{1,0:T(8,128)(2,1)} %bitcast.16, bf16[32,2,3,16,512]{4,3,2,1,0:T(8,128)(2,1)S(1)} %all-to-all-done.b_ref), custom_call_target="tpu_custom_call" | custom-call | tf_op jit(solution)/shard_map/terms/pallas_call | solution.py:137
  70.8 0.0 copy-start
  70.9 0.0 copy-start.1
  70.9 0.0 copy-start.2
  70.9 45.6 %all_to_all.15.blocks = bf16[32,2,3,16,512]{4,3,2,1,0:T(8,128)(2,1)S(1)} all-to-all(bf16[32,2,3,16,512]{4,3,2,1,0:T(8,128)(2,1)S(1)} %terms.1), channel_id=1, replica_groups=mesh['heads'=4,'seq'=32] {'seq'}, dimensions={0} | all-to-all | bytes 6291456 | tf_op jit(solution)/shard_map/all_to_all | solution.py:262
  116.5 0.0 copy-done
  116.5 0.0 copy-done.1
  116.5 0.0 copy-done.2
  116.5 5.0 %renew.1 = bf16[32,2,3,16,512]{4,3,2,1,0:T(8,128)(2,1)S(1)} custom-call(bf16[32,2,3,16,512]{4,3,2,1,0:T(8,128)(2,1)S(1)} %all_to_all.15.blocks, f32[2,16,512]{2,1,0:T(8,128)S(1)} %copy-done, f32[2,16,512]{2,1,0:T(8,128)S(1)} %copy-done.1, f32[2,16,512]{2,1,0:T(8,128)S(1)} %copy-done.2), custom_call_target="tpu_custom_call" | custom-call | tf_op jit(solution)/shard_map/renew/pallas_call | solution.py:71
  121.5 0.0 copy-start.3
  121.5 43.3 %all_to_all.16.c_ref = bf16[32,2,3,16,512]{4,3,2,1,0:T(8,128)(2,1)S(1)} all-to-all(bf16[32,2,3,16,512]{4,3,2,1,0:T(8,128)(2,1)S(1)} %renew.1), channel_id=1, replica_groups=mesh['heads'=4,'seq'=32] {'seq'}, dimensions={0} | all-to-all | bytes 6291456 | tf_op jit(solution)/shard_map/all_to_all | solution.py:262
  164.8 0.0 copy-done.3
  164.8 10.0 %apply.1 = (bf16[2048,1024]{1,0:T(8,128)(2,1)S(1)}, f32[1,2048]{1,0:T(1,128)S(1)}) custom-call(bf16[2048,1024]{1,0:T(8,128)(2,1)} %bitcast.18, bf16[32,2,3,16,512]{4,3,2,1,0:T(8,128)(2,1)S(1)} %all_to_all.16.c_ref, f32[2]{0:T(128)S(1)} %copy-done.3), custom_call_target="tpu_custom_call" | custom-call | tf_op jit(solution)/shard_map/apply/pallas_call | solution.py:187
  174.9 8.7 %all-gather.1.ssq_ref = f32[4,1,2048]{2,1,0:T(1,128)S(1)} all-gather(f32[1,1,2048]{2,1,0:T(1,128)S(1)} %bitcast.15), channel_id=2, replica_groups=mesh['heads'=4,'seq'=32] {'heads'}, dimensions={0}, use_global_device_ids=true | all-gather | bytes 40960 | tf_op jit(solution)/shard_map/all_gather | solution.py:282
  183.5 4.4 %finish.1 = bf16[16384,128]{1,0:T(8,128)(2,1)} custom-call(bf16[2048,1024]{1,0:T(8,128)(2,1)S(1)} %get-tuple-element.11.o_ref, f32[4,1,2048]{2,1,0:T(1,128)S(1)} %all-gather.1.ssq_ref, f32[2]{0:T(128)S(1)} %copy-done.3, s32[1]{0:T(128)} %dynamic_slice.3.live_ref), custom_call_target="tpu_custom_call" | custom-call | tf_op jit(solution)/shard_map/finish/pallas_call | solution.py:245
  (1 shorter events, 0.0 us)
Async XLA Ops:
  0.0 12.7 %copy-start.7 = (s32[32]{0:T(128)S(1)}, s32[32]{0:T(128)}, u32[]{:S(2)}) copy-start(s32[32]{0:T(128)} %param.13) | copy-start | bytes 388
  0.0 14.0 %copy-start.6 = (bf16[2,2048]{1,0:T(2,128)(2,1)S(1)}, bf16[2,2048]{1,0:T(2,128)(2,1)}, u32[]{:S(2)}) copy-start(bf16[2,2048]{1,0:T(2,128)(2,1)} %param.12) | copy-start | bytes 24580
  3.0 50.8 %all-to-all-start = ((bf16[32,2,3,16,512]{4,3,2,1,0:T(8,128)(2,1)}), bf16[32,2,3,16,512]{4,3,2,1,0:T(8,128)(2,1)S(1)}, u32[]{:S(2)}, u32[]{:S(2)}) async-start(bf16[32,2,3,16,512]{4,3,2,1,0:T(8,128)(2,1)} %spread.1), calls=%async_computation | async-start | bytes 6291456 | tf_op jit(solution)/shard_map/all_to_all | solution.py:262
  20.7 3.2 %copy-start.4 = (bf16[2048,2,512]{2,1,0:T(2,128)(2,1)S(1)}, bf16[2048,2,512]{2,1,0:T(2,128)(2,1)}, u32[]{:S(2)}) copy-start(bf16[2048,2,512]{2,1,0:T(2,128)(2,1)} %param.9) | copy-start | bytes 12582916
  23.9 3.2 %copy-start.5 = (bf16[2048,2,512]{2,1,0:T(2,128)(2,1)S(1)}, bf16[2048,2,512]{2,1,0:T(2,128)(2,1)}, u32[]{:S(2)}) copy-start(bf16[2048,2,512]{2,1,0:T(2,128)(2,1)} %param.10) | copy-start | bytes 12582916
  70.8 45.7 %copy-start = (f32[2,16,512]{2,1,0:T(8,128)S(1)}, f32[2,16,512]{2,1,0:T(8,128)}, u32[]{:S(2)}) copy-start(f32[2,16,512]{2,1,0:T(8,128)} %w_first.3) | copy-start | bytes 196612
  70.9 45.7 %copy-start.1 = (f32[2,16,512]{2,1,0:T(8,128)S(1)}, f32[2,16,512]{2,1,0:T(8,128)}, u32[]{:S(2)}) copy-start(f32[2,16,512]{2,1,0:T(8,128)} %w_third.3) | copy-start | bytes 196612
  70.9 45.7 %copy-start.2 = (f32[2,16,512]{2,1,0:T(8,128)S(1)}, f32[2,16,512]{2,1,0:T(8,128)}, u32[]{:S(2)}) copy-start(f32[2,16,512]{2,1,0:T(8,128)} %w_second.3) | copy-start | bytes 196612
  121.5 43.3 %copy-start.3 = (f32[2]{0:T(128)S(1)}, f32[2]{0:T(128)}, u32[]{:S(2)}) copy-start(f32[2]{0:T(128)} %scale_ref.3) | copy-start | bytes 28

commit v7 on v6

--- a/solution.py
+++ b/solution.py
@@ -53,8 +53,8 @@
     )(*weights)
 
 
-def renew_kernel(blocks, w_first, w_third, w_second, wide, chunk, sems):
-    groups = blocks.shape[1]
+def renew_kernel(blocks, w_first, w_third, w_second, wide):
+    peers, groups = blocks.shape[:2]
     for mat, ref in enumerate((w_first, w_third, w_second)):
         for group in range(groups):
             term = jnp.sum(blocks[:, group, mat].astype(jnp.float32), axis=0)
@@ -62,20 +62,16 @@
             update = start + term
             norm_old = jnp.mean(start * start, axis=-1, keepdims=True) + EPS
             norm_new = jnp.mean(update * update, axis=-1, keepdims=True) + EPS
-            fresh = update * (jnp.sqrt(norm_old) / jnp.sqrt(norm_new))
-            chunk[group, mat] = fresh.astype(jnp.bfloat16)
-    send_all(chunk, wide, sems)
+            fresh = (update * (jnp.sqrt(norm_old) / jnp.sqrt(norm_new))).astype(jnp.bfloat16)
+            for peer in range(peers):
+                wide[peer, group, mat] = fresh
 
 
 def renew(blocks, weights):
     return pl.pallas_call(
         renew_kernel,
-        out_specs=pl.BlockSpec(memory_space=pl.ANY),
+        out_specs=pl.BlockSpec(memory_space=pltpu.VMEM),
         out_shape=jax.ShapeDtypeStruct(blocks.shape, jnp.bfloat16),
-        scratch_shapes=[
-            pltpu.VMEM(blocks.shape[1:], jnp.bfloat16),
-            pltpu.SemaphoreType.DMA(blocks.shape[:1]),
-        ],
         compiler_params=params(24),
         name="renew",
     )(blocks, *weights)

time: 188 us -> 184 us (0.979)
  Pallas kernels: 39.4 us -> 35.1 us
    pallas_call x1, Pallas kernels: 4.95 us -> 0.69 us  [renew(): pl.pallas_call(renew_kernel, out_specs=pl.BlockSpec(memory_space=pltpu.VM...]
  transfers between devices with their start and end apart: 1 -> 1, of which waited for: 1 -> 1; matrix products, arithmetic and copies ran while one was open for 9% -> 10% of each run, Pallas kernels for 0% -> 0%
where the time goes in v7:
time: 184 us
  blocking collectives  97.7 us (53%)
  Pallas kernels  35.1 us (19%)
  waiting for transfers between devices  23.5 us (13%)
  local copies, waits for them, and re-layouts  11.6 us (6%)
  starting transfers between devices  9.74 us (5%)
  other arithmetic  5.99 us (3%)
    all_to_all x2, blocking collectives, exchange(): return lax.all_to_all(blocks, 'seq', 0, 0, tiled=True)  89 us
    all_to_all x1, waiting for transfers between devices, exchange(): return lax.all_to_all(blocks, 'seq', 0, 0, tiled=True)  23.5 us
    pallas_call x1, Pallas kernels, terms(): pl.pallas_call(terms_kernel, in_specs=[pl.BlockSpec(memory_space=pl.ANY),...  17.1 us
    pallas_call x1, Pallas kernels, apply(): pl.pallas_call(apply_kernel, grid=(steps,), in_specs=[tokens, pl.BlockSpe...  9.99 us
    all_to_all x1, starting transfers between devices, exchange(): return lax.all_to_all(blocks, 'seq', 0, 0, tiled=True)  9.74 us
    unnamed x19, local copies, waits for them, and re-layouts  9.58 us
    all_gather x1, blocking collectives, shards(): total_sq = lax.all_gather(partial_sq, 'heads', axis=0)  8.75 us
    convert_element_type x1, other arithmetic, shards(): (eta[:, :, None] * value_rows.astype(jnp.float32)).astype(jnp.bfloat16)  5.35 us
  transfers between devices with their start and end apart: 1, of which 1 were waited for; matrix products, arithmetic and copies ran while one was open for 10% of the time, Pallas kernels for 0%

profile of v7, /device:TPU:1, one launch (start us, length us, event | category | flops | bytes accessed | tf_op | source)
XLA Modules:
  0.0 183.7 jit_solution(16477727654734233337)
XLA Ops:
  0.0 0.0 copy-start.7
  0.0 0.0 copy-start.6
  0.0 2.9 %spread.1 = bf16[32,2,3,16,512]{4,3,2,1,0:T(8,128)(2,1)} custom-call(f32[2,16,512]{2,1,0:T(8,128)} %w_first.3, f32[2,16,512]{2,1,0:T(8,128)} %w_third.3, f32[2,16,512]{2,1,0:T(8,128)} %w_second.3), custom_call_target="tpu_custom_call" | custom-call | tf_op jit(solution)/shard_map/spread/pallas_call | solution.py:43
  3.0 9.7 %all-to-all-start = ((bf16[32,2,3,16,512]{4,3,2,1,0:T(8,128)(2,1)}), bf16[32,2,3,16,512]{4,3,2,1,0:T(8,128)(2,1)S(1)}, u32[]{:S(2)}, u32[]{:S(2)}) async-start(bf16[32,2,3,16,512]{4,3,2,1,0:T(8,128)(2,1)} %spread.1), calls=%async_computation | async-start | bytes 6291456 | tf_op jit(solution)/shard_map/all_to_all | solution.py:258
  12.7 0.0 copy-done.7
  12.7 0.6 dynamic_slice.3.live_ref
  13.4 0.6 fusion
  14.0 0.0 copy-done.6
  14.0 1.3 copy.12
  15.4 5.4 %multiply_convert_fusion = bf16[2048,2,512]{2,1,0:T(2,128)(2,1)S(1)} fusion(bf16[2048,2,512]{2,1,0:T(2,128)(2,1)} %param.11, f32[2048,2]{1,0:T(8,128)} %copy.12), kind=kLoop, calls=%fused_computation | loop fusion | flops 6291456 | bytes 8404992 | tf_op jit(solution)/shard_map/convert_element_type | solution.py:272
  20.7 0.0 copy-start.4
  20.7 3.2 %copy.16 = bf16[256,8,2,512]{3,1,2,0:T(8,128)(2,1)} copy(bf16[256,8,2,512]{3,2,1,0:T(2,128)(2,1)S(1)} %bitcast.19) | data formatting | bytes 8388608
  23.9 0.0 copy-done.4
  23.9 0.0 copy-start.5
  23.9 3.2 %copy.14 = bf16[256,8,2,512]{3,1,2,0:T(8,128)(2,1)} copy(bf16[256,8,2,512]{3,2,1,0:T(2,128)(2,1)S(1)} %bitcast.20) | data formatting | bytes 8388608
  27.1 0.0 copy-done.5
  27.1 3.1 %copy.15 = bf16[256,8,2,512]{3,1,2,0:T(8,128)(2,1)} copy(bf16[256,8,2,512]{3,2,1,0:T(2,128)(2,1)S(1)} %bitcast.21) | data formatting | bytes 8388608
  30.3 23.5 %all-to-all-done.b_ref = bf16[32,2,3,16,512]{4,3,2,1,0:T(8,128)(2,1)S(1)} async-done(((bf16[32,2,3,16,512]{4,3,2,1,0:T(8,128)(2,1)}), bf16[32,2,3,16,512]{4,3,2,1,0:T(8,128)(2,1)S(1)}, u32[]{:S(2)}, u32[]{:S(2)}) %all-to-all-start) | async-done | bytes 3145760 | tf_op jit(solution)/shard_map/all_to_all | solution.py:258
  53.8 17.1 %terms.1 = bf16[32,2,3,16,512]{4,3,2,1,0:T(8,128)(2,1)S(1)} custom-call(bf16[2048,1024]{1,0:T(8,128)(2,1)} %bitcast.17, bf16[2048,1024]{1,0:T(8,128)(2,1)} %bitcast.16, bf16[32,2,3,16,512]{4,3,2,1,0:T(8,128)(2,1)S(1)} %all-to-all-done.b_ref), custom_call_target="tpu_custom_call" | custom-call | tf_op jit(solution)/shard_map/terms/pallas_call | solution.py:133
  70.8 0.0 copy-start
  70.9 0.0 copy-start.1
  70.9 0.0 copy-start.2
  70.9 45.6 %all_to_all.15.blocks = bf16[32,2,3,16,512]{4,3,2,1,0:T(8,128)(2,1)S(1)} all-to-all(bf16[32,2,3,16,512]{4,3,2,1,0:T(8,128)(2,1)S(1)} %terms.1), channel_id=1, replica_groups=mesh['heads'=4,'seq'=32] {'seq'}, dimensions={0} | all-to-all | bytes 6291456 | tf_op jit(solution)/shard_map/all_to_all | solution.py:258
  116.5 0.0 copy-done
  116.5 0.0 copy-done.1
  116.5 0.0 copy-done.2
  116.5 0.7 renew.1
  117.2 0.0 copy-start.3
  117.2 43.3 %all_to_all.16.c_ref = bf16[32,2,3,16,512]{4,3,2,1,0:T(8,128)(2,1)S(1)} all-to-all(bf16[32,2,3,16,512]{4,3,2,1,0:T(8,128)(2,1)S(1)} %renew.1), channel_id=1, replica_groups=mesh['heads'=4,'seq'=32] {'seq'}, dimensions={0} | all-to-all | bytes 6291456 | tf_op jit(solution)/shard_map/all_to_all | solution.py:258
  160.6 0.0 copy-done.3
  160.6 10.0 %apply.1 = (bf16[2048,1024]{1,0:T(8,128)(2,1)S(1)}, f32[1,2048]{1,0:T(1,128)S(1)}) custom-call(bf16[2048,1024]{1,0:T(8,128)(2,1)} %bitcast.18, bf16[32,2,3,16,512]{4,3,2,1,0:T(8,128)(2,1)S(1)} %all_to_all.16.c_ref, f32[2]{0:T(128)S(1)} %copy-done.3), custom_call_target="tpu_custom_call" | custom-call | tf_op jit(solution)/shard_map/apply/pallas_call | solution.py:183
  170.6 8.7 %all-gather.1.ssq_ref = f32[4,1,2048]{2,1,0:T(1,128)S(1)} all-gather(f32[1,1,2048]{2,1,0:T(1,128)S(1)} %bitcast.15), channel_id=2, replica_groups=mesh['heads'=4,'seq'=32] {'heads'}, dimensions={0}, use_global_device_ids=true | all-gather | bytes 40960 | tf_op jit(solution)/shard_map/all_gather | solution.py:278
  179.3 4.4 %finish.1 = bf16[16384,128]{1,0:T(8,128)(2,1)} custom-call(bf16[2048,1024]{1,0:T(8,128)(2,1)S(1)} %get-tuple-element.11.o_ref, f32[4,1,2048]{2,1,0:T(1,128)S(1)} %all-gather.1.ssq_ref, f32[2]{0:T(128)S(1)} %copy-done.3, s32[1]{0:T(128)} %dynamic_slice.3.live_ref), custom_call_target="tpu_custom_call" | custom-call | tf_op jit(solution)/shard_map/finish/pallas_call | solution.py:241
  (1 shorter events, 0.0 us)
Async XLA Ops:
  0.0 12.7 %copy-start.7 = (s32[32]{0:T(128)S(1)}, s32[32]{0:T(128)}, u32[]{:S(2)}) copy-start(s32[32]{0:T(128)} %param.13) | copy-start | bytes 388
  0.0 14.0 %copy-start.6 = (bf16[2,2048]{1,0:T(2,128)(2,1)S(1)}, bf16[2,2048]{1,0:T(2,128)(2,1)}, u32[]{:S(2)}) copy-start(bf16[2,2048]{1,0:T(2,128)(2,1)} %param.12) | copy-start | bytes 24580
  3.0 50.8 %all-to-all-start = ((bf16[32,2,3,16,512]{4,3,2,1,0:T(8,128)(2,1)}), bf16[32,2,3,16,512]{4,3,2,1,0:T(8,128)(2,1)S(1)}, u32[]{:S(2)}, u32[]{:S(2)}) async-start(bf16[32,2,3,16,512]{4,3,2,1,0:T(8,128)(2,1)} %spread.1), calls=%async_computation | async-start | bytes 6291456 | tf_op jit(solution)/shard_map/all_to_all | solution.py:258
  20.7 3.2 %copy-start.4 = (bf16[2048,2,512]{2,1,0:T(2,128)(2,1)S(1)}, bf16[2048,2,512]{2,1,0:T(2,128)(2,1)}, u32[]{:S(2)}) copy-start(bf16[2048,2,512]{2,1,0:T(2,128)(2,1)} %param.9) | copy-start | bytes 12582916
  23.9 3.2 %copy-start.5 = (bf16[2048,2,512]{2,1,0:T(2,128)(2,1)S(1)}, bf16[2048,2,512]{2,1,0:T(2,128)(2,1)}, u32[]{:S(2)}) copy-start(bf16[2048,2,512]{2,1,0:T(2,128)(2,1)} %param.10) | copy-start | bytes 12582916
  70.8 45.7 %copy-start = (f32[2,16,512]{2,1,0:T(8,128)S(1)}, f32[2,16,512]{2,1,0:T(8,128)}, u32[]{:S(2)}) copy-start(f32[2,16,512]{2,1,0:T(8,128)} %w_first.3) | copy-start | bytes 196612
  70.9 45.7 %copy-start.1 = (f32[2,16,512]{2,1,0:T(8,128)S(1)}, f32[2,16,512]{2,1,0:T(8,128)}, u32[]{:S(2)}) copy-start(f32[2,16,512]{2,1,0:T(8,128)} %w_third.3) | copy-start | bytes 196612
  70.9 45.7 %copy-start.2 = (f32[2,16,512]{2,1,0:T(8,128)S(1)}, f32[2,16,512]{2,1,0:T(8,128)}, u32[]{:S(2)}) copy-start(f32[2,16,512]{2,1,0:T(8,128)} %w_second.3) | copy-start | bytes 196612
  117.2 43.3 %copy-start.3 = (f32[2]{0:T(128)S(1)}, f32[2]{0:T(128)}, u32[]{:S(2)}) copy-start(f32[2]{0:T(128)} %scale_ref.3) | copy-start | bytes 28
